TPU v7x, 32 devices: a whole 2x2x4 slice. The times are simulated.
32 devices in a mesh: rows: 8 (over z, x), seq: 4 (over y, core).
Axes of the slice: x: 2, y: 2, z: 4, core: 2. Of those that a mesh axis runs over, the one named last changes fastest.
Arguments:
- layer_input: float32 [8, 1024, 768], P('rows', 'seq'), may hold values from -6 to 6
- doc_lengths: int32 [8, 4], P('rows'), may hold values from 1 to 976, as said below
- output_grad: float32 [8, 1024, 768], P('rows', 'seq'), may hold values from -6 to 6
- mixer_gain: float32 [768], replicated, may hold values from 0.5 to 1.5
- triple_weight: float32 [768, 2304], replicated, may hold values from -0.21875 to 0.21875
- rate_weight: float32 [768, 12], replicated, may hold values from -0.21875 to 0.21875
- rate_bias: float32 [12], replicated, may hold values from -3 to 3
- first_weight: float32 [12, 64, 256], replicated, may hold values from -0.75 to 0.75
- first_bias: float32 [12, 256], replicated, may hold values from -3 to 3
- second_weight: float32 [12, 256, 64], replicated, may hold values from -0.375 to 0.375
- second_bias: float32 [12, 64], replicated, may hold values from -3 to 3
- inner_gain: float32 [12, 64], replicated, may hold values from 0.5 to 1.5
- inner_shift: float32 [12, 64], replicated, may hold values from -3 to 3
- gate_weight: float32 [768, 768], replicated, may hold values from -0.21875 to 0.21875
- output_weight: float32 [768, 768], replicated, may hold values from -0.21875 to 0.21875
- feed_gain: float32 [768], replicated, may hold values from 0.5 to 1.5
- feed_weight: float32 [768, 4096], replicated, may hold values from -0.21875 to 0.21875
- down_weight: float32 [2048, 768], replicated, may hold values from -0.125 to 0.125
Outputs:
- layer_output: float32 [8, 1024, 768], P('rows', 'seq')
- input_grad: float32 [8, 1024, 768], P('rows', 'seq')
- mixer_gain_grad: float32 [768], replicated
- triple_weight_grad: float32 [768, 2304], P('rows', 'seq')
- rate_weight_grad: float32 [768, 12], replicated
- rate_bias_grad: float32 [12], replicated
- first_weight_grad: float32 [12, 64, 256], replicated
- first_bias_grad: float32 [12, 256], replicated
- second_weight_grad: float32 [12, 256, 64], replicated
- second_bias_grad: float32 [12, 64], replicated
- inner_gain_grad: float32 [12, 64], replicated
- inner_shift_grad: float32 [12, 64], replicated
- gate_weight_grad: float32 [768, 768], P('rows', 'seq')
- output_weight_grad: float32 [768, 768], P('rows', 'seq')
- feed_gain_grad: float32 [768], replicated
- feed_weight_grad: float32 [768, 4096], P('rows', 'seq')
- down_weight_grad: float32 [2048, 768], P('rows', 'seq')
Inputs may be any that keep to these rules, and one draw needn't show every extreme that they name: `doc_lengths`: each row holds 4 documents in order, each starting on a multiple of 16 tokens and taking ceil(length / 16) whole mini-batches; together they take exactly the row's 1024 / 16 mini-batches. The second document of every row starts in the row's first 256 tokens and ends in its last 256.
All inputs are finite; a program needn't handle non-finite values.
Results may differ from a plain program's by a relative error of at most 0.0003.
Values sent between devices are 32-bit elements; how exact they have to be, the bound alone decides.
No kernel may reach another device: no remote copies, remote signals or barrier semaphores. Data moves between devices by JAX's collectives and lax.ppermute only.
A program may use at most 256 MiB of HBM per device.

v0:
```python
import jax
import jax.numpy as jnp
from jax import lax
from jax.sharding import PartitionSpec as P

HEADS = 12
HEAD = 64
INNER = 256
MB = 16


highest = lax.Precision.HIGHEST
base_rate = 0.1
epsilon = 1e-06
root_two_pi = 0.7978845608028654


def passed_along(value, axis, steps):
    count = lax.axis_size(axis)
    leading, last = (max(0, -steps), min(count, count - steps))
    return lax.ppermute(value, axis, [(source, source + steps) for source in range(leading, last)])


def gelu_tanh(value_in):
    cubic = root_two_pi * (value_in + 0.044715 * value_in * value_in * value_in)
    return 0.5 * value_in * (1.0 + jnp.tanh(cubic))


def gelu_slope(value_in):
    tangent = jnp.tanh(root_two_pi * (value_in + 0.044715 * value_in * value_in * value_in))
    return 0.5 * (1.0 + tangent) + 0.5 * value_in * (1.0 - tangent * tangent) * root_two_pi * (
        1.0 + 0.134145 * value_in * value_in
    )


def rms_scale(value_in, norm_gain):
    return (
        value_in
        * lax.rsqrt(jnp.mean(value_in * value_in, axis=-1, keepdims=True) + epsilon)
        * norm_gain
    )


def layer_norm(value_in):
    centered = value_in - jnp.mean(value_in, axis=-1, keepdims=True)
    inverse = lax.rsqrt(jnp.mean(centered * centered, axis=-1, keepdims=True) + epsilon)
    return (centered * inverse, inverse)


def inner_step(carried, minibatch, initial, norm_pair):
    query_heads, key_heads, value_heads, rate_vals, reset_flag = minibatch
    carried = tuple(
        (
            reset_flag * learned + (1.0 - reset_flag) * current
            for learned, current in zip(initial, carried)
        )
    )
    weight_in, bias_in, weight_out, bias_out = carried
    norm_gain = norm_pair[0][:, None, :]
    norm_shift = norm_pair[1][:, None, :]
    pre_hidden = (
        jnp.einsum("htk,hki->hti", key_heads, weight_in, precision=highest) + bias_in[:, None, :]
    )
    activated = gelu_tanh(pre_hidden)
    pre_out = (
        jnp.einsum("hti,hik->htk", activated, weight_out, precision=highest) + bias_out[:, None, :]
    )
    normed, inverse = layer_norm(pre_out)
    target = value_heads - key_heads
    scaled = (norm_gain * normed + norm_shift - target) * norm_gain
    out_grad = inverse * (
        scaled
        - jnp.mean(scaled, axis=-1, keepdims=True)
        - normed * jnp.mean(scaled * normed, axis=-1, keepdims=True)
    )
    hidden_grad = jnp.einsum("htk,hik->hti", out_grad, weight_out, precision=highest) * gelu_slope(
        pre_hidden
    )
    length = query_heads.shape[1]
    causal = jnp.tril(jnp.ones((length, length), jnp.float32))
    step_rates = causal[None, :, :] * rate_vals[:, None, :]
    query_key = jnp.einsum("htk,hsk->hts", query_heads, key_heads, precision=highest) + 1.0
    query_pre = (
        jnp.einsum("htk,hki->hti", query_heads, weight_in, precision=highest)
        + bias_in[:, None, :]
        - jnp.einsum("hts,hsi->hti", step_rates * query_key, hidden_grad, precision=highest)
    )
    query_act = gelu_tanh(query_pre)
    query_act_key = jnp.einsum("hti,hsi->hts", query_act, activated, precision=highest) + 1.0
    query_out = (
        jnp.einsum("hti,hik->htk", query_act, weight_out, precision=highest)
        + bias_out[:, None, :]
        - jnp.einsum("hts,hsk->htk", step_rates * query_act_key, out_grad, precision=highest)
    )
    query_norm = layer_norm(query_out)[0]
    result = query_heads + norm_gain * query_norm + norm_shift
    rated_hidden = rate_vals[:, :, None] * hidden_grad
    rated_out = rate_vals[:, :, None] * out_grad
    updated = (
        weight_in - jnp.einsum("htk,hti->hki", key_heads, rated_hidden, precision=highest),
        bias_in - jnp.sum(rated_hidden, axis=1),
        weight_out - jnp.einsum("hti,htk->hik", activated, rated_out, precision=highest),
        bias_out - jnp.sum(rated_out, axis=1),
    )
    return (updated, result)


def doc_masks(lengths, offset, span):
    block_counts = (lengths + MB - 1) // MB
    begins = jnp.cumsum(block_counts, dtype=jnp.int32) - block_counts
    block_index = offset // MB + jnp.arange(span // MB, dtype=jnp.int32)
    resets = jnp.any(block_index[:, None] == begins[None, :], axis=1).astype(jnp.float32)
    positions = offset + jnp.arange(span, dtype=jnp.int32)
    starts = begins * MB
    inside = (positions[:, None] >= starts[None, :]) & (
        positions[:, None] < (starts + lengths)[None, :]
    )
    return (resets, jnp.any(inside, axis=1).astype(jnp.float32))


def pack_state(carried):
    return jnp.concatenate([member.reshape(-1) for member in carried])


def unpack_state(flat):
    first_size = HEADS * HEAD * INNER
    bias_size = HEADS * INNER
    weight_in = flat[:first_size].reshape(HEADS, HEAD, INNER)
    bias_in = flat[first_size : first_size + bias_size].reshape(HEADS, INNER)
    second_start = first_size + bias_size
    weight_out = flat[second_start : second_start + first_size].reshape(HEADS, INNER, HEAD)
    bias_out = flat[second_start + first_size :].reshape(HEADS, HEAD)
    return (weight_in, bias_in, weight_out, bias_out)


def local(
    layer_input,
    doc_lengths,
    output_grad,
    mixer_gain,
    triple_weight,
    rate_weight,
    rate_bias,
    first_weight,
    first_bias,
    second_weight,
    second_bias,
    inner_gain,
    inner_shift,
    gate_weight,
    output_weight,
    feed_gain,
    feed_weight,
    down_weight,
):
    row_count, group_len, width = layer_input.shape
    block_count = group_len // MB
    state_size = HEADS * (2 * HEAD * INNER + INNER + HEAD)
    seq_total = lax.axis_size("seq")
    offset = lax.axis_index("seq") * group_len

    def row_masks(lengths):
        return doc_masks(lengths, offset, group_len)

    resets, valid_mask = jax.vmap(row_masks)(doc_lengths)

    def arrange(columns):
        return columns.reshape(row_count, block_count, MB, HEADS, HEAD).transpose(0, 1, 3, 2, 4)

    def prepare(pre_params, tokens):
        norm_gain, triple_mat, rate_mat, rate_shift, gate_mat = pre_params
        normed = rms_scale(tokens, norm_gain)
        triple = jnp.einsum("rtd,de->rte", normed, triple_mat, precision=highest)
        rate_vals = (
            base_rate
            / HEAD
            * jax.nn.sigmoid(
                jnp.einsum("rtd,dh->rth", normed, rate_mat, precision=highest) + rate_shift
            )
            * valid_mask[:, :, None]
        )
        rate_vals = rate_vals.reshape(row_count, block_count, MB, HEADS).transpose(0, 1, 3, 2)
        gate_pre = jnp.einsum("rtd,de->rte", normed, gate_mat, precision=highest)
        features = (
            arrange(triple[:, :, :width]),
            arrange(triple[:, :, width : 2 * width]),
            arrange(triple[:, :, 2 * width :]),
            rate_vals,
        )
        return (features, gate_pre)

    def chain(inner_params, features, start_state):
        initial = inner_params[:4]
        norm_pair = inner_params[4:]

        def step(carried, minibatch):
            return inner_step(carried, minibatch, initial, norm_pair)

        checked = jax.checkpoint(step)

        def one_row(row_features, row_resets, row_start):
            final_state, results = lax.scan(
                checked, unpack_state(row_start), row_features + (row_resets,)
            )
            return (results, pack_state(final_state))

        return jax.vmap(one_row)(features, resets, start_state)

    def finish(post_params, tokens, results, gate_pre):
        projection, second_norm, expand, contract = post_params
        mixed_heads = results.transpose(0, 1, 3, 2, 4).reshape(row_count, group_len, width)
        gated_mix = gelu_tanh(gate_pre) * mixed_heads
        middle = tokens + jnp.einsum("rtd,de->rte", gated_mix, projection, precision=highest)
        normed = rms_scale(middle, second_norm)
        both = jnp.einsum("rtd,df->rtf", normed, expand, precision=highest)
        half_width = expand.shape[1] // 2
        hidden = jax.nn.silu(both[:, :, :half_width]) * both[:, :, half_width:]
        return middle + jnp.einsum("rtf,fd->rtd", hidden, contract, precision=highest)

    pre_params = (mixer_gain, triple_weight, rate_weight, rate_bias, gate_weight)
    inner_params = (first_weight, first_bias, second_weight, second_bias, inner_gain, inner_shift)
    post_params = (output_weight, feed_gain, feed_weight, down_weight)
    (features, gate_pre), pre_pullback = jax.vjp(prepare, pre_params, layer_input)

    def forward_turn(turn_index, start_state):
        end_states = chain(inner_params, features, start_state)[1]
        return passed_along(end_states, "seq", 1)

    start_state = lax.fori_loop(
        0, seq_total - 1, forward_turn, jnp.zeros((row_count, state_size), jnp.float32)
    )
    chain_out, chain_pullback = jax.vjp(chain, inner_params, features, start_state)
    results = chain_out[0]
    layer_output, post_pullback = jax.vjp(finish, post_params, layer_input, results, gate_pre)
    post_grads, input_late, result_grad, gate_grad = post_pullback(output_grad)

    def backward_once(end_grad):
        return chain_pullback((result_grad, end_grad))

    def backward_turn(turn_index, end_grad):
        start_grad = backward_once(end_grad)[2]
        return passed_along(start_grad, "seq", -1)

    end_grad = lax.fori_loop(
        0, seq_total - 1, backward_turn, jnp.zeros((row_count, state_size), jnp.float32)
    )
    chain_grads = backward_once(end_grad)
    inner_grads = chain_grads[0]
    feature_grads = chain_grads[1]
    pre_grads, input_early = pre_pullback((feature_grads, gate_grad))
    input_grad = input_early + input_late
    reduced = (
        lax.psum_scatter(pre_grads[1], "seq", scatter_dimension=1, tiled=True),
        lax.psum_scatter(pre_grads[4], "seq", scatter_dimension=1, tiled=True),
        lax.psum_scatter(post_grads[0], "seq", scatter_dimension=1, tiled=True),
        lax.psum_scatter(post_grads[2], "seq", scatter_dimension=1, tiled=True),
        lax.psum_scatter(post_grads[3], "seq", scatter_dimension=1, tiled=True),
    )
    reduced = (
        lax.psum_scatter(reduced[0], "rows", scatter_dimension=0, tiled=True),
        lax.psum_scatter(reduced[1], "rows", scatter_dimension=0, tiled=True),
        lax.psum_scatter(reduced[2], "rows", scatter_dimension=0, tiled=True),
        lax.psum_scatter(reduced[3], "rows", scatter_dimension=0, tiled=True),
        lax.psum_scatter(reduced[4], "rows", scatter_dimension=0, tiled=True),
    )
    summed = lax.psum(
        (
            pre_grads[0],
            pre_grads[2],
            pre_grads[3],
            inner_grads[0],
            inner_grads[1],
            inner_grads[2],
            inner_grads[3],
            inner_grads[4],
            inner_grads[5],
            post_grads[1],
        ),
        ("rows", "seq"),
    )
    return (
        layer_output,
        input_grad,
        summed[0],
        reduced[0],
        summed[1],
        summed[2],
        summed[3],
        summed[4],
        summed[5],
        summed[6],
        summed[7],
        summed[8],
        reduced[1],
        reduced[2],
        summed[9],
        reduced[3],
        reduced[4],
    )


def solution(mesh):
    in_specs = (
        P("rows", "seq", None),
        P("rows", None),
        P("rows", "seq", None),
        P(),
        P(),
        P(),
        P(),
        P(),
        P(),
        P(),
        P(),
        P(),
        P(),
        P(),
        P(),
        P(),
        P(),
        P(),
    )
    out_specs = (
        P("rows", "seq", None),
        P("rows", "seq", None),
        P(),
        P("rows", "seq"),
        P(),
        P(),
        P(),
        P(),
        P(),
        P(),
        P(),
        P(),
        P("rows", "seq"),
        P("rows", "seq"),
        P(),
        P("rows", "seq"),
        P("rows", "seq"),
    )
    return jax.shard_map(local, mesh=mesh, in_specs=in_specs, out_specs=out_specs, check_vma=False)
```

profile of v0, /device:TPU:0, one launch (start us, length us, event | category | flops | bytes accessed | tf_op | source)
XLA Modules:
  0.0 4866.4 jit_solution(17160933177450165138)
XLA Ops:
  14.1 8.3 convolution_bitcast_fusion.36
  37.1 1128.0 %while.160 = (s32[]{:T(128)}, f32[1,397056]{1,0:T(1,128)}, f32[1,16,12,16,64]{4,3,2,1,0:T(8,128)}, f32[1,16,12,16,64]{4,3,2,1,0:T(8,128)}, f32[1,16,12,16]{3,2,1...) while((s32[]{:T(128)}, f32[1,397056]{1,0:T(1,128)}, ...), condition=%wide.region_13.14_spmd, body=%wide.region_4.13_spmd.sunk | while | flops 194234304 | bytes 40016496 | solution.py:229
  37.3 10.5 slice_reduce_fusion.22
  56.8 313.2 %while.165 = (s32[]{:T(128)}, f32[1,12,64,256]{3,2,1,0:T(8,128)}, f32[1,12,256]{2,1,0:T(8,128)S(1)}, f32[1,12,256,64]{2,3,1,0:T(8,128)}, f32[1,12,64]{2,1,0:T(8,...) while((s32[]{:T(128)}, f32[1,12,64,256]{3,2,1,0:T(8,128)}, ...), condition=%wide.region_12.12_spmd, body=%wide.region_5.11_spmd.sunk | while | flops 193043136 | bytes 17811724 | solution.py:202
  69.5 4.2 fusion.854
  89.1 4.2 fusion.854
  108.7 4.2 fusion.854
  128.2 4.2 fusion.854
  147.8 4.2 fusion.854
  167.4 4.2 fusion.854
  187.0 4.2 fusion.854
  226.1 4.2 fusion.854
  324.0 4.2 fusion.854
  379.0 17.4 pad_maximum_fusion.2
  402.1 10.5 slice_reduce_fusion.22
  421.6 313.2 %while.165 = (s32[]{:T(128)}, f32[1,12,64,256]{3,2,1,0:T(8,128)}, f32[1,12,256]{2,1,0:T(8,128)S(1)}, f32[1,12,256,64]{2,3,1,0:T(8,128)}, f32[1,12,64]{2,1,0:T(8,...) while((s32[]{:T(128)}, f32[1,12,64,256]{3,2,1,0:T(8,128)}, ...), condition=%wide.region_12.12_spmd, body=%wide.region_5.11_spmd.sunk | while | flops 193043136 | bytes 17811724 | solution.py:202
  493.0 4.2 fusion.854
  590.9 4.2 fusion.854
  649.6 4.2 fusion.854
  708.4 4.2 fusion.854
  743.8 17.4 pad_maximum_fusion.2
  761.1 20.2 collective-permute-start.1
  783.5 10.5 slice_reduce_fusion.22
  803.0 313.2 %while.165 = (s32[]{:T(128)}, f32[1,12,64,256]{3,2,1,0:T(8,128)}, f32[1,12,256]{2,1,0:T(8,128)S(1)}, f32[1,12,256,64]{2,3,1,0:T(8,128)}, f32[1,12,64]{2,1,0:T(8,...) while((s32[]{:T(128)}, f32[1,12,64,256]{3,2,1,0:T(8,128)}, ...), condition=%wide.region_12.12_spmd, body=%wide.region_5.11_spmd.sunk | while | flops 193043136 | bytes 17811724 | solution.py:202
  815.7 4.2 fusion.854
  894.0 4.2 fusion.854
  991.9 4.2 fusion.854
  1050.6 4.2 fusion.854
  1125.2 17.4 pad_maximum_fusion.2
  1142.5 20.0 collective-permute-start.1
  1165.1 10.5 slice_reduce_fusion.10
  1197.8 465.0 %while.163 = (s32[]{:T(128)}, f32[1,12,64,256]{3,2,1,0:T(8,128)}, f32[1,12,256]{2,1,0:T(8,128)S(1)}, f32[1,12,256,64]{2,3,1,0:T(8,128)}, f32[1,12,64]{2,1,0:T(8,...) while((s32[]{:T(128)}, f32[1,12,64,256]{3,2,1,0:T(8,128)}, ...), condition=%wide.region_23.24_spmd.clone, body=%wide.region_14.23_spmd.clone.sunk | while | flops 292631936 | bytes 28750176 | solution.py:202
  1675.8 14.0 convolution_bitcast_fusion.35
  1689.8 9.9 fusion.467
  1699.8 11.5 fusion.423
  1716.5 4.6 fusion.452
  1727.4 10.4 fusion.399
  1743.4 1791.2 %while.162 = (s32[]{:T(128)}, f32[1,397056]{1,0:T(1,128)}, f32[1,16,12,16,64]{4,3,2,1,0:T(8,128)}, f32[16,1,12,64,256]{4,3,2,1,0:T(8,128)}, f32[16,1,12,256]{3,2...) while((s32[]{:T(128)}, f32[1,397056]{1,0:T(1,128)}, ...), condition=%wide.region_46.47_spmd, body=%wide.region_26.46_spmd.sunk | while | flops 677630912 | bytes 69306968 | solution.py:244
  1762.4 10.2 slice_reduce_fusion.25
  1777.1 525.5 %while.166 = (s32[]{:T(128)}, f32[1,12,64,256]{3,2,1,0:T(8,128)}, f32[1,12,256]{2,1,0:T(8,128)S(1)}, f32[1,12,256,64]{2,3,1,0:T(8,128)S(1)}, f32[1,12,64]{2,1,0:...) while((s32[]{:T(128)}, f32[1,12,64,256]{3,2,1,0:T(8,128)}, ...), condition=%wide.region_45.45_spmd, body=%wide.region_27.44_spmd.sunk | while | flops 676439744 | bytes 37603432 | solution.py:202
  2307.1 22.9 pad_add_fusion.8
  2331.2 20.7 collective-permute-done
  2353.1 10.2 slice_reduce_fusion.25
  2367.8 524.9 %while.166 = (s32[]{:T(128)}, f32[1,12,64,256]{3,2,1,0:T(8,128)}, f32[1,12,256]{2,1,0:T(8,128)S(1)}, f32[1,12,256,64]{2,3,1,0:T(8,128)S(1)}, f32[1,12,64]{2,1,0:...) while((s32[]{:T(128)}, f32[1,12,64,256]{3,2,1,0:T(8,128)}, ...), condition=%wide.region_45.45_spmd, body=%wide.region_27.44_spmd.sunk | while | flops 676439744 | bytes 37603432 | solution.py:202
  2897.3 22.9 pad_add_fusion.8
  2921.4 21.3 collective-permute-done
  2943.9 10.2 slice_reduce_fusion.25
  2958.6 524.9 %while.166 = (s32[]{:T(128)}, f32[1,12,64,256]{3,2,1,0:T(8,128)}, f32[1,12,256]{2,1,0:T(8,128)S(1)}, f32[1,12,256,64]{2,3,1,0:T(8,128)S(1)}, f32[1,12,64]{2,1,0:...) while((s32[]{:T(128)}, f32[1,12,64,256]{3,2,1,0:T(8,128)}, ...), condition=%wide.region_45.45_spmd, body=%wide.region_27.44_spmd.sunk | while | flops 676439744 | bytes 37603432 | solution.py:202
  3488.1 22.9 pad_add_fusion.8
  3512.2 20.8 collective-permute-done
  3534.6 10.2 slice_reduce_fusion.8
  3559.4 739.5 %while.164 = (s32[]{:T(128)}, f32[12,64,256]{2,1,0:T(8,128)}, f32[12,256]{1,0:T(8,128)}, f32[12,256,64]{1,2,0:T(8,128)}, f32[12,64]{1,0:T(8,128)}, /*index=5*/f3...) while((s32[]{:T(128)}, f32[12,64,256]{2,1,0:T(8,128)}, ...), condition=%wide.region_73.74_spmd.clone, body=%wide.region_47.73_spmd.clone.sunk | while | flops 805051520 | bytes 65395528 | solution.py:202
  4308.9 15.0 fusion.393
  4325.0 15.0 fusion.389
  4346.1 59.0 %reduce-scatter.17.cloned.1.call-done = f32[768,576]{0,1:T(8,128)} async-done(((f32[768,2304]{0,1:T(8,128)}), f32[768,576]{0,1:T(8,128)}) %reduce-scatter.17.cloned.1.call-update) | async-done | bytes 1769488 | tf_op jit(solution)/shard_map/reduce_scatter | solution.py:253
  4407.9 99.4 %reduce-scatter.23.cloned.1.call-done = f32[768,1024]{1,0:T(8,128)} async-done(((f32[768,4096]{1,0:T(8,128)}), f32[768,1024]{1,0:T(8,128)}) %reduce-scatter.23.cloned.1.call-update) | async-done | bytes 3145744 | tf_op jit(solution)/shard_map/reduce_scatter | solution.py:256
  4508.5 5.1 fusion.464
  4513.6 8.5 fusion.395
  4523.4 41.8 all-reduce.9
  4566.3 11.7 fusion.409
  4578.0 62.1 %reduce-scatter.33.cloned.1.call-done = f32[96,192]{1,0:T(8,128)} async-done(((f32[768,192]{1,0:T(8,128)}), f32[96,192]{1,0:T(8,128)}) %reduce-scatter.33.cloned.1.call-update) | async-done | bytes 73744
  4640.1 68.4 %reduce-scatter.29.cloned.1.call-done = f32[256,192]{0,1:T(8,128)} async-done(((f32[2048,192]{0,1:T(8,128)}), f32[256,192]{0,1:T(8,128)}) %reduce-scatter.29.cloned.1.call-update) | async-done | bytes 196624 | tf_op jit(solution)/shard_map/reduce_scatter | solution.py:264
  4708.5 70.0 %reduce-scatter.31.cloned.1.call-done = f32[96,576]{1,0:T(8,128)} async-done(((f32[768,576]{1,0:T(8,128)}), f32[96,576]{1,0:T(8,128)}) %reduce-scatter.31.cloned.1.call-update) | async-done | bytes 221200
  4778.5 77.3 %reduce-scatter.25.cloned.1.call-done = f32[96,1024]{1,0:T(8,128)} async-done(((f32[768,1024]{1,0:T(8,128)}), f32[96,1024]{1,0:T(8,128)}) %reduce-scatter.25.cloned.1.call-update) | async-done | bytes 393232 | tf_op jit(solution)/shard_map/reduce_scatter | solution.py:263
  (7071 shorter events, 3776.6 us)
Async XLA Ops:
  8.0 1665.2 %copy-start = (f32[768,768]{1,0:T(8,128)S(1)}, f32[768,768]{1,0:T(8,128)}, u32[]{:S(2)}) copy-start(f32[768,768]{1,0:T(8,128)} %param.44) | copy-start | bytes 7077892
  8.0 4332.6 %reduce-scatter.21.cloned.1.call-start = ((), (), s32[]{:S(2)}) async-start(), calls=%async_computation.12 | async-start | bytes 2949120 | tf_op jit(solution)/shard_map/reduce_scatter | solution.py:255
  11.2 11.2 copy-start.82
  11.3 11.1 copy-start.84
  11.3 11.1 copy-start.73
  396.4 5.7 collective-permute-start.1
  761.1 22.4 collective-permute-start.1
  1142.5 22.2 collective-permute-start.1
  1673.2 38.4 copy-start.37
  1675.7 35.6 copy-start.26
  1675.8 35.6 copy-start.77
  1675.8 14.0 copy-start.54
  1675.8 24.0 slice-start
  1675.8 24.0 slice-start.1
  1689.8 9.9 copy-start.47
  1689.8 10.0 slice-start.2
  1699.8 11.6 copy-start.40
  1699.8 11.6 copy-start.41
  1716.4 2626.6 %reduce-scatter.19.cloned.1.call-start = ((), (), s32[]{:S(2)}) async-start(), calls=%async_computation.11 | async-start | bytes 2949120 | tf_op jit(solution)/shard_map/reduce_scatter | solution.py:254
  1726.3 2619.1 %reduce-scatter.27.cloned.1.call-start = ((), (), s32[]{:S(2)}) async-start(), calls=%async_computation.15 | async-start | bytes 7864320 | tf_op jit(solution)/shard_map/reduce_scatter | solution.py:257
  1737.8 2667.2 %reduce-scatter.17.cloned.1.call-start = ((), (), s32[]{:S(2)}) async-start(), calls=%async_computation.10 | async-start | bytes 8847360 | tf_op jit(solution)/shard_map/reduce_scatter | solution.py:253
  2329.9 22.0 collective-permute-start
  2920.1 22.6 collective-permute-start
  3510.9 22.1 collective-permute-start
  3559.6 9.1 copy-start.80
  3574.5 10.9 copy-start.22
  3619.0 10.9 copy-start.22
  3665.3 10.9 copy-start.22
  3696.7 9.1 copy-start.80
  3711.6 11.0 copy-start.22
  3742.9 9.1 copy-start.80
  3757.9 10.9 copy-start.22
  3789.2 9.1 copy-start.80
  3804.2 10.9 copy-start.22
  3835.5 9.1 copy-start.80
  3850.5 10.9 copy-start.22
  3881.8 9.1 copy-start.80
  3896.8 10.9 copy-start.22
  3928.1 9.1 copy-start.80
  3943.1 10.9 copy-start.22
  3974.4 9.1 copy-start.80
  3989.4 11.0 copy-start.22
  4035.7 10.9 copy-start.22
  4067.0 9.1 copy-start.80
  4082.0 10.9 copy-start.22
  4113.3 9.1 copy-start.80
  4128.3 10.9 copy-start.22
  4174.6 11.0 copy-start.22
  4220.9 11.0 copy-start.22
  4267.2 11.0 copy-start.22
  4323.9 183.4 %reduce-scatter.23.cloned.1.call-start = ((), (), s32[]{:S(2)}) async-start(), calls=%async_computation.13 | async-start | bytes 15728640 | tf_op jit(solution)/shard_map/reduce_scatter | solution.py:256
  4340.0 237.9 %all-reduce.13.cloned.1.call-start = ((), (), s32[]{:S(2)}) async-start(), calls=%async_computation.20 | async-start | bytes 3145728 | tf_op jit(solution)/shard_map/psum | solution.py:266
  4340.6 237.4 %reduce-scatter.35.cloned.1.call-start = ((), (), s32[]{:S(2)}) async-start(), calls=%async_computation.19 | async-start | bytes 884736
  4342.9 297.1 %reduce-scatter.33.cloned.1.call-start = ((), (), s32[]{:S(2)}) async-start(), calls=%async_computation.18 | async-start | bytes 884736
  4345.3 363.2 %reduce-scatter.29.cloned.1.call-start = ((), (), s32[]{:S(2)}) async-start(), calls=%async_computation.16 | async-start | bytes 1769472 | tf_op jit(solution)/shard_map/reduce_scatter | solution.py:264
  4346.0 432.5 %reduce-scatter.31.cloned.1.call-start = ((), (), s32[]{:S(2)}) async-start(), calls=%async_computation.17 | async-start | bytes 2211840
  4407.8 99.5 %copy-start.85 = (pred[256]{0:T(512)(128)(4,1)S(1)}, pred[256]{0:T(512)(128)(4,1)}, u32[]{:S(2)}) copy-start(pred[256]{0:T(512)(128)(4,1)} %copy-done.84) | copy-start | bytes 772
  4407.9 99.6 %copy-start.62 = (f32[16,1,12,16]{3,1,2,0:T(1,128)S(1)}, f32[16,1,12,16]{3,1,2,0:T(1,128)}, u32[]{:S(2)}) copy-start(f32[16,1,12,16]{3,1,2,0:T(1,128)} %get-tuple-element.1808) | copy-start | bytes 36868
  4407.9 99.7 %copy-start.76 = (f32[256,12]{0,1:T(8,128)S(1)}, f32[256,12]{0,1:T(8,128)}, u32[]{:S(2)}) copy-start(f32[256,12]{0,1:T(8,128)} %get-tuple-element.2770) | copy-start | bytes 36868
  4407.9 447.9 %reduce-scatter.25.cloned.1.call-start = ((), (), s32[]{:S(2)}) async-start(), calls=%async_computation.14 | async-start | bytes 3538944 | tf_op jit(solution)/shard_map/reduce_scatter | solution.py:263
  4522.2 43.0 copy-start.83
  4522.2 43.0 copy-start.36
  4566.3 292.4 %copy-start.1 = (f32[768,768]{1,0:T(8,128)S(1)}, f32[768,768]{1,0:T(8,128)}, u32[]{:S(2)}) copy-start(f32[768,768]{1,0:T(8,128)} %param.44) | copy-start | bytes 7077892
  4578.0 279.9 %copy-start.53 = (f32[12,256,64]{1,2,0:T(8,128)S(1)}, f32[12,256,64]{1,2,0:T(8,128)}, u32[]{:S(2)}) copy-start(f32[12,256,64]{1,2,0:T(8,128)} %get-tuple-element.4278) | copy-start | bytes 2359300
  (577 other events, 2602.0 us)
Sparse Core Ops, SparseCore 0:
  1716.5 52.0 reduce-scatter.20
  1771.3 33.0 reduce-scatter.18
  1807.0 58.4 reduce-scatter.26
  4324.1 80.9 reduce-scatter.16
  4407.5 99.8 reduce-scatter.22
  4511.1 62.6 reduce-scatter.34
  4578.6 61.4 reduce-scatter.32
  4644.1 64.3 reduce-scatter.28
  4712.9 65.5 reduce-scatter.30
  4782.5 73.2 reduce-scatter.24
Sparse Core Ops, SparseCore 1:
  4346.0 217.8 all-reduce.12
where the time goes:
time: 4920 us; the launch traced here: 4870 us
  matrix products  2230 us (45%)
  other arithmetic  1140 us (23%)
  local copies, waits for them, and re-layouts  783 us (16%)
  waiting for transfers between devices  507 us (10%)
  loops' own time  103 us (2%)
    squeeze x448, local copies, waits for them, and re-layouts, one_row(): lax.scan(checked, unpack_state(row_start), row_features + (row_resets,))  415 us
    dot_general x144, matrix products, inner_step(): jnp.einsum('htk,hti->hki', key_heads, rated_hidden, precision=highest)  350 us
    dot_general x208, matrix products, inner_step(): jnp.einsum('htk,hki->hti', key_heads, weight_in, precision=highest)  314 us
    dot_general x160, matrix products, inner_step(): jnp.einsum('htk,hki->hti', query_heads, weight_in, precision=highest)  279 us
    dot_general x256, matrix products, inner_step(): jnp.einsum('htk,hik->hti', out_grad, weight_out, precision=highest)  241 us
    dot_general x256, matrix products, inner_step(): jnp.einsum('hti,hik->htk', activated, weight_out, precision=highest)  241 us
    dot_general x192, matrix products, inner_step(): jnp.einsum('hti,htk->hik', activated, rated_out, precision=highest)  212 us
    add x160, other arithmetic, inner_step(): reset_flag * learned + (1.0 - reset_flag) * current  193 us

commit v1 on v0

v1 whole, which is shorter than its diff:
```python
import functools
import jax
import jax.numpy as jnp
from jax import lax
from jax.experimental import pallas as pl
from jax.experimental.pallas import tpu as pltpu
from jax.sharding import PartitionSpec as P

HEAD = 64
INNER = 256
MB = 16
EPS = 1e-06
RTP = 0.7978845608028654
F32 = jnp.float32
BF16 = jnp.bfloat16
LANES = 128


def hi_lo(value):
    high = value.astype(BF16)
    return high, (value - high.astype(F32)).astype(BF16)


def mm(left, right):
    return lax.dot_general(left, right, (((1,), (0,)), ((), ())), preferred_element_type=F32)


def mm_nt(left, right):
    return lax.dot_general(left, right, (((1,), (1,)), ((), ())), preferred_element_type=F32)


def mm_tn(left, right):
    return lax.dot_general(left, right, (((0,), (0,)), ((), ())), preferred_element_type=F32)


def rows2(*parts):
    return jnp.concatenate(parts, axis=0)


def fold(value):
    return value[:MB] + value[MB:]


def half_turn(value):
    return pltpu.roll(value, HEAD, 1)


def both_halves(value):
    return value + half_turn(value)


def lane_of(shape):
    return lax.broadcasted_iota(jnp.int32, shape, 1)


def pick(block, unit):
    tile = block[:, (unit // 2) * LANES : (unit // 2 + 1) * LANES]
    turned = half_turn(tile)
    low_half = lane_of(tile.shape) < HEAD
    if unit % 2 == 0:
        return jnp.where(low_half, tile, turned)
    return jnp.where(low_half, turned, tile)


def pack(parts):
    tiles = []
    for at in range(0, len(parts), 2):
        left = parts[at]
        right = parts[at + 1] if at + 1 < len(parts) else jnp.zeros_like(left)
        tiles.append(jnp.where(lane_of(left.shape) < HEAD, left, right))
    return jnp.concatenate(tiles, axis=1) if len(tiles) > 1 else tiles[0]


def mean_dup(value):
    return jnp.sum(value, axis=1, keepdims=True) * (1.0 / LANES)


def gelu_parts(z):
    z2 = z * z
    t = jnp.tanh(z * (RTP + (RTP * 0.044715) * z2))
    one_t = 0.5 + 0.5 * t
    sech = (1.0 - t) * one_t
    inner = RTP + (RTP * 0.134145) * z2
    act = z * one_t
    zs = z * sech
    slope = one_t + zs * inner
    return act, slope, t, zs, sech, inner


def gelu_curve(z, t, zs, sech, inner):
    return 2.0 * sech * inner + zs * ((2.0 * RTP * 0.134145) * z) - 2.0 * t * zs * inner * inner


def split3(high, low):
    return rows2(high, high, low)


def stack3(high, low):
    return rows2(high, low, high)


def lanes3(value):
    high, low = hi_lo(value)
    lane = lane_of(value.shape)
    return jnp.where((lane >= MB) & (lane < 2 * MB), low.astype(F32), high.astype(F32)).astype(BF16)


def fwd_kernel(heads, steps, resets_ref, qkv_ref, rate_ref, gain_ref, shift_ref, w1i, b1i, w2i, b2i,
               out_ref, s1_ref, s2_ref, z1_ref, zq_ref, m_ref, d2_ref, x_ref, y_ref, r_ref, rq_ref,
               w1, b1, w2, b2):
    block = pl.program_id(0)

    def step(i, carry):
        at = block * steps + i

        @pl.when(resets_ref[at] == 1)
        def _():
            w1[...] = w1i[...]
            b1[...] = b1i[...]
            w2[...] = w2i[...]
            b2[...] = b2i[...]

        rows = pl.ds(pl.multiple_of(i * MB, MB), MB)
        qkv = qkv_ref[rows, :]
        rates = rate_ref[rows, :]
        lane = lane_of((MB, LANES))
        row = lax.broadcasted_iota(jnp.int32, (MB, LANES), 0)
        outs = []
        for h in range(heads):
            gain = gain_ref[h]
            shift = shift_ref[h]
            q = pick(qkv, h)
            k = pick(qkv, heads + h)
            v = pick(qkv, 2 * heads + h)
            e = jnp.broadcast_to(rates[:, h : h + 1], (MB, LANES))
            coef = gain * (shift - v + k)
            coef_mean = mean_dup(coef)
            gain2 = gain * gain
            khi, klo = hi_lo(k)
            qhi, qlo = hi_lo(q)
            left_a = rows2(khi, klo, qhi, qlo)
            qsplit = jnp.where(lane < HEAD, qhi.astype(F32), qlo.astype(F32)).astype(BF16)
            zero = jnp.zeros((HEAD, LANES), BF16)
            kq = fold(mm_nt(rows2(khi, klo), rows2(zero, qsplit, zero[: HEAD - MB])))
            causal = (lane >= HEAD) & (lane < HEAD + MB) & (row <= lane - HEAD)
            left_d = e * jnp.where(lane < HEAD, k, jnp.where(causal, kq + 1.0, jnp.where((lane >= HEAD + MB) & (lane < HEAD + 2 * MB), 1.0, 0.0)))
            left_d3 = jnp.transpose(stack3(*hi_lo(left_d)))[: HEAD + 2 * MB]
            erow = jnp.transpose(e)[:MB, :]
            erow3 = jnp.concatenate([erow, erow, erow], axis=1)
            lane48 = lane_of((MB, 3 * MB))
            row48 = lax.broadcasted_iota(jnp.int32, (MB, 3 * MB), 0)
            e3 = jnp.where(lax.rem(lane48, MB) <= row48, erow3, 0.0)

            w1f = w1[h]
            w2f = w2[h]
            w1s = rows2(*hi_lo(w1f))
            w2s = rows2(*hi_lo(w2f))
            s1_ref[i, h] = w1s
            s2_ref[i, h] = w2s
            b1v = b1[h]
            b2v = b2[h]
            z = mm(left_a, w1s)
            z1 = z[:MB] + z[MB : 2 * MB] + b1v
            act, slope = gelu_parts(z1)[:2]
            ahi, alo = hi_lo(act)
            left_b = rows2(ahi, alo)
            z2 = both_halves(fold(mm_nt(left_b, w2s))) + b2v
            g2z = gain2 * z2
            inv = lax.rsqrt(mean_dup(z2 * z2) + EPS)
            m1 = mean_dup(g2z)
            m2 = mean_dup(g2z * z2)
            m3 = mean_dup(coef * z2)
            x = z2 * inv
            g = gain2 * x + coef
            d2 = inv * (g - (inv * m1 + coef_mean) - x * (inv * inv * m2 + inv * m3))
            d2hi, d2lo = hi_lo(d2)
            m = fold(mm(rows2(d2hi, d2lo), w2s))
            d1 = m * slope
            u = mm(left_d3, split3(*hi_lo(d1)))
            w1[h] = w1f - u[:HEAD]
            b1[h] = b1v - u[HEAD + MB :]
            zq = z[2 * MB : 3 * MB] + z[3 * MB :] + b1v - u[HEAD : HEAD + MB]
            qact = gelu_parts(zq)[0]
            qahi, qalo = hi_lo(qact)
            left_e = rows2(qahi, qalo)
            uq = fold(mm_nt(left_e, rows2(ahi, ahi, ahi))) + mm_nt(qahi, rows2(alo, alo, alo))
            r3 = lanes3(e3 * (uq + 1.0))
            z2q = both_halves(fold(mm_nt(left_e, w2s))) + b2v - mm(r3, split3(d2hi, d2lo))
            invq = lax.rsqrt(mean_dup(z2q * z2q) + EPS)
            y = z2q * invq
            outs.append(q + gain * y + shift)
            ed2 = e * d2
            upd = mm(jnp.transpose(stack3(*hi_lo(ed2)))[:HEAD], split3(ahi, alo))
            w2[h] = w2f - upd
            b2[h] = b2v - jnp.sum(ed2, axis=0, keepdims=True)
            z1_ref[i, h] = z1
            zq_ref[i, h] = zq
            m_ref[i, h] = m
            d2_ref[i, h] = d2
            x_ref[i, h] = x
            y_ref[i, h] = y
            r_ref[i, h] = jnp.broadcast_to(inv, (MB, LANES))
            rq_ref[i, h] = jnp.broadcast_to(invq, (MB, LANES))
        out_ref[rows, :] = pack(outs)
        return carry

    lax.fori_loop(0, steps, step, 0)


def bwd_kernel(heads, steps, resets_ref, qkv_ref, rate_ref, cot_ref, gain_ref, shift_ref,
               s1_ref, s2_ref, z1_ref, zq_ref, m_ref, d2_ref, x_ref, y_ref, r_ref, rq_ref,
               dqkv_ref, de_ref, gw1, gb1, gw2, gb2, ggain, gshift,
               w1, b1, w2, b2):
    blocks = pl.num_programs(0)
    block = blocks - 1 - pl.program_id(0)

    @pl.when(pl.program_id(0) == 0)
    def _():
        for ref in (gw1, gb1, gw2, gb2, ggain, gshift, w1, b1, w2, b2):
            ref[...] = jnp.zeros_like(ref)

    def step(back, carry):
        i = steps - 1 - back
        at = block * steps + i
        rows = pl.ds(pl.multiple_of(i * MB, MB), MB)
        qkv = qkv_ref[rows, :]
        rates = rate_ref[rows, :]
        cots = cot_ref[rows, :]
        lane = lane_of((MB, LANES))
        lane48 = lane_of((MB, 3 * MB))
        row48 = lax.broadcasted_iota(jnp.int32, (MB, 3 * MB), 0)
        causal3 = row48 <= lax.rem(lane48, MB)
        dqs, dks, dvs = [], [], []
        de_all = jnp.zeros((MB, LANES), F32)
        for h in range(heads):
            gain = gain_ref[h]
            shift = shift_ref[h]
            gain2 = gain * gain
            q = pick(qkv, h)
            k = pick(qkv, heads + h)
            v = pick(qkv, 2 * heads + h)
            cot = pick(cots, h)
            ecol = rates[:, h : h + 1]
            e = jnp.broadcast_to(ecol, (MB, LANES))
            e256 = jnp.broadcast_to(ecol, (MB, INNER))
            e3 = jnp.where(causal3, jnp.broadcast_to(ecol, (MB, 3 * MB)), 0.0)
            khi, klo = hi_lo(k)
            qhi, qlo = hi_lo(q)
            left_k = rows2(khi, klo)
            qsplit = jnp.where(lane < HEAD, qhi.astype(F32), qlo.astype(F32)).astype(BF16)
            kq3 = fold(mm_nt(left_k, rows2(qsplit, qsplit, qsplit))) + 1.0
            pt3 = lanes3(e3 * kq3)
            ones = jnp.where(lane < HEAD + MB, 1.0, 0.0)
            qone = hi_lo(jnp.where(lane < HEAD, q, ones))
            kone = hi_lo(jnp.where(lane < HEAD, k, ones))
            left_q = jnp.transpose(rows2(stack3(*qone), stack3(*kone)))[: HEAD + MB]

            s1 = s1_ref[i, h]
            s2 = s2_ref[i, h]
            z1 = z1_ref[i, h]
            zq = zq_ref[i, h]
            m = m_ref[i, h]
            d2 = d2_ref[i, h]
            x = x_ref[i, h]
            y = y_ref[i, h]
            inv = r_ref[i, h]
            invq = rq_ref[i, h]
            act, slope, t, zs, sech, inner = gelu_parts(z1)
            curve = gelu_curve(z1, t, zs, sech, inner)
            qact, qslope = gelu_parts(zq)[:2]
            ahi, alo = hi_lo(act)
            qahi, qalo = hi_lo(qact)
            d1 = m * slope

            dy = gain * cot
            dz2q = invq * (dy - mean_dup(dy) - y * mean_dup(dy * y))
            ggain_part = cot * y
            zhi, zlo = hi_lo(dz2q)
            dqa = fold(mm(rows2(zhi, zlo), s2))
            left_a = rows2(ahi, alo)
            aq3 = fold(mm_nt(left_a, rows2(qahi, qahi, qahi))) + mm_nt(ahi, rows2(qalo, qalo, qalo)) + 1.0
            rt3 = lanes3(e3 * aq3)
            d2hi, d2lo = hi_lo(d2)
            zsplit = jnp.where(lane < HEAD, zhi.astype(F32), zlo.astype(F32)).astype(BF16)
            drt3 = -fold(mm_nt(rows2(d2hi, d2lo), rows2(zsplit, zsplit, zsplit)))
            third = lane48 < MB
            de = jnp.sum(jnp.where(causal3 & third, drt3 * aq3, 0.0), axis=1, keepdims=True)
            du2t = e3 * drt3
            du2t_hi, du2t_lo = hi_lo(du2t[:, :MB])
            dqa = dqa + mm_tn(rows2(du2t_hi, du2t_lo, du2t_hi), split3(ahi, alo))
            da = mm(lanes3(du2t), split3(qahi, qalo))
            dzq = dqa * qslope
            zqhi, zqlo = hi_lo(dzq)
            d1hi, d1lo = hi_lo(d1)
            dpt3 = -(fold(mm_nt(rows2(d1hi, d1lo), rows2(zqhi, zqhi, zqhi))) + mm_nt(d1hi, rows2(zqlo, zqlo, zqlo)))
            de = de + jnp.sum(jnp.where(causal3 & third, dpt3 * kq3, 0.0), axis=1, keepdims=True)
            du1t = e3 * dpt3
            du1t_hi, du1t_lo = hi_lo(du1t[:, :MB])
            dq = cot + mm_tn(rows2(du1t_hi, du1t_lo, du1t_hi), split3(khi, klo))
            dk = mm(lanes3(du1t), split3(qhi, qlo))
            zq3 = split3(zqhi, zqlo)
            dd1 = -mm(pt3, zq3)
            dd2 = -mm(rt3, split3(zhi, zlo))

            w1f = w1[h]
            w2f = w2[h]
            b1v = b1[h]
            b2v = b2[h]
            w1s = rows2(*hi_lo(w1f))
            w2s = rows2(*hi_lo(w2f))
            de1 = -(fold(mm(left_k, w1s)) + b1v)
            de = de + jnp.sum(d1 * de1, axis=1, keepdims=True)
            dd1 = dd1 + e256 * de1
            ed1 = e256 * d1
            dkw = -fold(mm_nt(rows2(*hi_lo(ed1)), w1s))
            de2 = -(both_halves(fold(mm_nt(left_a, w2s))) + b2v)
            de = de + 0.5 * jnp.sum(d2 * de2, axis=1, keepdims=True)
            ed2 = e * d2
            da = da - fold(mm(rows2(*hi_lo(ed2)), w2s))
            dm = dd1 * slope
            dz1 = dd1 * m * curve
            dmhi, dmlo = hi_lo(dm)
            dd2 = dd2 + e * de2 + both_halves(fold(mm_nt(rows2(dmhi, dmlo), s2)))

            coef = gain * (shift - v + k)
            g = gain2 * x + coef
            mg = mean_dup(g)
            mgx = mean_dup(g * x)
            q1 = mean_dup(dd2)
            q2 = mean_dup(dd2 * x)
            dr_r = 2.0 * HEAD * 0.5 * mean_dup(dd2 * d2)
            dg = inv * (dd2 - q1 - x * q2)
            dx = dg * gain2 - inv * (dd2 * mgx + g * q2)
            ggain_part = ggain_part + dg * (2.0 * gain * x + shift - v + k)
            dgg = dg * gain
            dz2 = inv * (dx - mean_dup(dx) - x * mean_dup(dx * x)) - x * inv * (dr_r * (1.0 / HEAD))
            dz2hi, dz2lo = hi_lo(dz2)
            da = da + fold(mm(rows2(dz2hi, dz2lo), s2))
            dz1 = dz1 + da * slope
            z1hi, z1lo = hi_lo(dz1)
            grads = mm(left_q, rows2(zq3, split3(z1hi, z1lo)))
            to_rows = mm_nt(rows2(zqhi, zqlo, z1hi, z1lo), s1)
            dq = dq + both_halves(fold(to_rows[: 2 * MB]))
            dk = dk + dgg + both_halves(dkw + fold(to_rows[2 * MB :]))
            left_2 = jnp.transpose(rows2(stack3(zhi, zlo), stack3(d2hi, d2lo), stack3(dz2hi, dz2lo)))[:HEAD]
            grads2 = mm(left_2, rows2(split3(qahi, qalo), split3(dmhi, dmlo), split3(ahi, alo)))
            w1[h] = w1f + grads[:HEAD]
            b1[h] = b1v + grads[HEAD:]
            w2[h] = w2f + grads2
            b2[h] = b2v + jnp.sum(dz2q + dz2, axis=0, keepdims=True)
            ggain[h] += ggain_part
            gshift[h] += cot + dgg
            dqs.append(dq)
            dks.append(dk)
            dvs.append(-dgg)
            de_all = jnp.where(lane == h, de, de_all)
        dqkv_ref[rows, :] = pack(dqs + dks + dvs)
        de_ref[rows, :] = de_all

        @pl.when(resets_ref[at] == 1)
        def _():
            gw1[...] += w1[...]
            gb1[...] += b1[...]
            gw2[...] += w2[...]
            gb2[...] += b2[...]
            for ref in (w1, b1, w2, b2):
                ref[...] = jnp.zeros_like(ref)

        return carry

    lax.fori_loop(0, steps, step, 0)


def tiles_of(count):
    return -(-count // 2) * LANES


def state_scratch(heads):
    return [
        pltpu.VMEM((heads, HEAD, INNER), F32),
        pltpu.VMEM((heads, MB, INNER), F32),
        pltpu.VMEM((heads, HEAD, INNER), F32),
        pltpu.VMEM((heads, MB, LANES), F32),
    ]


def saved_shapes(total, heads):
    return [
        ((total, heads, LANES, INNER), BF16),
        ((total, heads, LANES, INNER), BF16),
        ((total, heads, MB, INNER), F32),
        ((total, heads, MB, INNER), F32),
        ((total, heads, MB, INNER), F32),
        ((total, heads, MB, LANES), F32),
        ((total, heads, MB, LANES), F32),
        ((total, heads, MB, LANES), F32),
        ((total, heads, MB, LANES), F32),
        ((total, heads, MB, LANES), F32),
    ]


def whole_spec(shape):
    zeros = (0,) * len(shape)
    return pl.BlockSpec(shape, lambda i, *_: zeros)


def chain_forward(resets, qkv, rates, gain, shift, w1i, b1i, w2i, b2i, steps=8, interpret=False):
    heads = gain.shape[0]
    total = resets.shape[0]
    blocks = total // steps
    token_spec = lambda width: pl.BlockSpec((steps * MB, width), lambda i, *_: (i, 0))
    saved = saved_shapes(total, heads)
    saved_specs = [pl.BlockSpec((steps,) + s[1:], lambda i, *_: (i, 0, 0, 0)) for s, _ in saved]
    params = (gain, shift, w1i, b1i, w2i, b2i)
    out = pl.pallas_call(
        functools.partial(fwd_kernel, heads, steps),
        grid_spec=pltpu.PrefetchScalarGridSpec(
            num_scalar_prefetch=1,
            grid=(blocks,),
            in_specs=[token_spec(qkv.shape[1]), token_spec(LANES)] + [whole_spec(p.shape) for p in params],
            out_specs=[token_spec(tiles_of(heads))] + saved_specs,
            scratch_shapes=state_scratch(heads),
        ),
        out_shape=[jax.ShapeDtypeStruct((total * MB, tiles_of(heads)), F32)] + [jax.ShapeDtypeStruct(s, d) for s, d in saved],
        compiler_params=pltpu.CompilerParams(dimension_semantics=("arbitrary",), vmem_limit_bytes=56 * 1024 * 1024),
        interpret=interpret,
    )(resets, qkv, rates, *params)
    return out[0], out[1:]


def chain_backward(resets, qkv, rates, cot, gain, shift, saved, steps=8, interpret=False):
    heads = gain.shape[0]
    total = resets.shape[0]
    blocks = total // steps
    token_spec = lambda width: pl.BlockSpec((steps * MB, width), lambda i, *_: (blocks - 1 - i, 0))
    saved_specs = [pl.BlockSpec((steps,) + s.shape[1:], lambda i, *_: (blocks - 1 - i, 0, 0, 0)) for s in saved]
    acc_shapes = [(heads, HEAD, INNER), (heads, MB, INNER), (heads, HEAD, INNER), (heads, MB, LANES), (heads, MB, LANES), (heads, MB, LANES)]
    return pl.pallas_call(
        functools.partial(bwd_kernel, heads, steps),
        grid_spec=pltpu.PrefetchScalarGridSpec(
            num_scalar_prefetch=1,
            grid=(blocks,),
            in_specs=[token_spec(qkv.shape[1]), token_spec(LANES), token_spec(cot.shape[1]), whole_spec(gain.shape), whole_spec(shift.shape)] + saved_specs,
            out_specs=[token_spec(qkv.shape[1]), token_spec(LANES)] + [whole_spec(s) for s in acc_shapes],
            scratch_shapes=state_scratch(heads),
        ),
        out_shape=[jax.ShapeDtypeStruct(qkv.shape, F32), jax.ShapeDtypeStruct((total * MB, LANES), F32)]
        + [jax.ShapeDtypeStruct(s, F32) for s in acc_shapes],
        compiler_params=pltpu.CompilerParams(dimension_semantics=("arbitrary",), vmem_limit_bytes=56 * 1024 * 1024),
        interpret=interpret,
    )(resets, qkv, rates, cot, gain, shift, *saved)


HEADS = 12
base_rate = 0.1
high = lax.Precision.HIGH


def dot(left, right):
    return jnp.dot(left, right, precision=high)


def dot_t(left, right):
    return lax.dot_general(left, right, (((1,), (1,)), ((), ())), precision=high)


def t_dot(left, right):
    return lax.dot_general(left, right, (((0,), (0,)), ((), ())), precision=high)


def swap(value, axis, mask):
    count = lax.axis_size(axis)
    return lax.ppermute(value, axis, [(source, source ^ mask) for source in range(count)])


def bits_of(axis):
    count = lax.axis_size(axis)
    return [1 << at for at in reversed(range(count.bit_length() - 1))]


def gather(value, axis):
    me = lax.axis_index(axis)
    shape = value.shape
    for done, mask in enumerate(bits_of(axis)):
        other = swap(value, axis, mask)
        upper = (me & mask) != 0
        value = jnp.stack([jnp.where(upper, other, value), jnp.where(upper, value, other)], axis=done)
    return value.reshape((-1,) + shape)


def scatter_sum(value, axis):
    me = lax.axis_index(axis)
    masks = bits_of(axis)
    value = value.reshape((2,) * len(masks) + value.shape[1:])
    for mask in reversed(masks):
        last = masks.index(mask)
        upper = (me & mask) != 0
        lower_half = lax.index_in_dim(value, 0, last, keepdims=False)
        upper_half = lax.index_in_dim(value, 1, last, keepdims=False)
        other = swap(jnp.where(upper, lower_half, upper_half), axis, mask)
        value = jnp.where(upper, upper_half, lower_half) + other
    return value


def sum_over(value, axis):
    for mask in reversed(bits_of(axis)):
        value = value + swap(value, axis, mask)
    return value


def columns_to_tokens(value, groups, width):
    n = lax.axis_size("seq")
    tokens = value.shape[0] // n
    moved = lax.all_to_all(value.reshape(n, tokens, -1), "seq", 0, 0)
    moved = moved.reshape(n, tokens, groups, -1).transpose(1, 2, 0, 3)
    return moved.reshape(tokens, groups, -1)[:, :, :width]


def tokens_to_columns(value):
    n = lax.axis_size("seq")
    tokens = value.shape[0]
    moved = lax.all_to_all(value.reshape(tokens, n, -1).transpose(1, 0, 2), "seq", 0, 0)
    return moved.reshape(n * tokens, -1)


def doc_masks(lengths, span):
    block_counts = (lengths + MB - 1) // MB
    begins = jnp.cumsum(block_counts, dtype=jnp.int32) - block_counts
    block_index = jnp.arange(span // MB, dtype=jnp.int32)
    resets = jnp.any(block_index[:, None] == begins[None, :], axis=1).astype(jnp.int32)
    positions = jnp.arange(span, dtype=jnp.int32)
    starts = begins * MB
    inside = (positions[:, None] >= starts[None, :]) & (positions[:, None] < (starts + lengths)[None, :])
    return resets, jnp.any(inside, axis=1).astype(F32)


def own_heads(value, axis, per_head, groups=1):
    n = lax.axis_size("seq")
    me = lax.axis_index("seq")
    count = -(-HEADS // n)
    shape = value.shape
    value = value.reshape(shape[:axis] + (groups, HEADS * per_head) + shape[axis + 1 :])
    pads = [(0, 0)] * value.ndim
    pads[axis + 1] = (0, (n * count - HEADS) * per_head)
    value = jnp.pad(value, pads)
    value = lax.dynamic_slice_in_dim(value, me * count * per_head, count * per_head, axis + 1)
    return value.reshape(shape[:axis] + (groups * count * per_head,) + shape[axis + 1 :])


def pad_columns(value, width):
    return jnp.pad(value, ((0, 0), (0, width - value.shape[1])))


def local(
    layer_input,
    doc_lengths,
    output_grad,
    mixer_gain,
    triple_weight,
    rate_weight,
    rate_bias,
    first_weight,
    first_bias,
    second_weight,
    second_bias,
    inner_gain,
    inner_shift,
    gate_weight,
    output_weight,
    feed_gain,
    feed_weight,
    down_weight,
):
    n = lax.axis_size("seq")
    n_rows = lax.axis_size("rows")
    me = lax.axis_index("seq")
    heads = -(-HEADS // n)
    _, tokens, width = layer_input.shape
    span = tokens * n
    ff = down_weight.shape[0]
    x = layer_input[0]
    cot = output_grad[0]
    resets, valid = doc_masks(doc_lengths[0], span)

    inv = lax.rsqrt(jnp.mean(x * x, axis=-1, keepdims=True) + EPS)
    xhat = x * inv
    normed = xhat * mixer_gain
    normed_row = gather(normed, "seq").reshape(span, width)
    own_triple = own_heads(triple_weight, 1, HEAD, 3)
    own_gate = own_heads(gate_weight, 1, HEAD)
    own_rate = own_heads(rate_weight, 1, 1)
    qkv = dot(normed_row, pad_columns(own_triple, tiles_of(3 * heads)))
    rate_sig = jax.nn.sigmoid(dot(normed_row, pad_columns(own_rate, LANES)) + jnp.pad(own_heads(rate_bias, 0, 1), (0, LANES - heads)))
    rates = (base_rate / HEAD) * rate_sig * valid[:, None]

    def per_head(value, rows, axis):
        value = own_heads(value, 0, 1)
        return jnp.broadcast_to(jnp.concatenate([value] * axis, axis=1)[:, None, :], (heads, rows, value.shape[1] * axis))

    gain = per_head(inner_gain, MB, 2)
    shift = per_head(inner_shift, MB, 2)
    w1i = own_heads(first_weight, 0, 1)
    b1i = per_head(first_bias, MB, 1)
    w2t = own_heads(second_weight, 0, 1).transpose(0, 2, 1)
    w2i = w2t - jnp.mean(w2t, axis=1, keepdims=True)
    b2i = per_head(second_bias - jnp.mean(second_bias, axis=1, keepdims=True), MB, 2)
    mixed, saved = chain_forward(resets, qkv, rates, gain, shift, w1i, b1i, w2i, b2i)
    mixed = mixed[:, : heads * HEAD]

    gate_pre = dot(normed_row, own_gate)
    gate_act, gate_slope = gelu_parts(gate_pre)[:2]
    gated = columns_to_tokens(gate_act * mixed, 1, width)[:, 0]
    middle = x + dot(gated, output_weight)
    inv2 = lax.rsqrt(jnp.mean(middle * middle, axis=-1, keepdims=True) + EPS)
    mhat = middle * inv2
    second = mhat * feed_gain
    both = dot(second, feed_weight)
    left, right = both[:, :ff], both[:, ff:]
    sig = jax.nn.sigmoid(left)
    silu = left * sig
    hidden = silu * right
    layer_output = middle + dot(hidden, down_weight)

    dhidden = dot_t(cot, down_weight)
    dboth = jnp.concatenate([dhidden * right * (sig + silu * (1.0 - sig)), dhidden * silu], axis=1)
    dsecond = dot_t(dboth, feed_weight)
    feed_gain_part = jnp.sum(dsecond * mhat, axis=0)
    dmhat = dsecond * feed_gain
    dmiddle = cot + inv2 * (dmhat - mhat * jnp.mean(dmhat * mhat, axis=-1, keepdims=True))
    dgated = tokens_to_columns(pad_columns(dot_t(dmiddle, output_weight), n * heads * HEAD))
    dmixed = pad_columns(dgated * gate_act, tiles_of(heads))
    dgate = dgated * mixed * gate_slope

    second_row = gather(second, "seq").reshape(span, width)
    dboth_cols = tokens_to_columns(dboth)
    feed_part = t_dot(second_row, dboth_cols)
    down_part = scatter_sum(jnp.stack(jnp.split(t_dot(hidden, cot), n, axis=1)), "seq")
    output_part = scatter_sum(jnp.stack(jnp.split(t_dot(gated, dmiddle), n, axis=1)), "seq")

    def over_rows(part):
        return scatter_sum(part.reshape((n_rows, part.shape[0] // n_rows) + part.shape[1:]), "rows")

    feed_weight_grad = over_rows(feed_part)
    down_weight_grad = over_rows(down_part)
    output_weight_grad = over_rows(output_part)

    dqkv, drate, gw1, gb1, gw2, gb2, ggain, gshift = chain_backward(resets, qkv, rates, dmixed, gain, shift, saved)
    dqkv = dqkv[:, : 3 * heads * HEAD]
    dpre = drate[:, :heads] * rates[:, :heads] * (1.0 - rate_sig[:, :heads])

    dcols = jnp.concatenate([dqkv, dgate], axis=1)
    weights_part = t_dot(normed_row, dcols)
    rate_part = t_dot(normed_row, dpre)
    weights_sum = over_rows(weights_part)
    all_cols = gather(weights_sum, "seq").reshape(n, weights_sum.shape[0], 4, heads * HEAD)
    all_cols = all_cols.transpose(1, 2, 0, 3).reshape(weights_sum.shape[0], 4, -1)[:, :, :width]
    triple_all = all_cols[:, :3].reshape(weights_sum.shape[0], 3 * width)
    triple_weight_grad = lax.dynamic_slice_in_dim(triple_all, me * (3 * width // n), 3 * width // n, 1)
    gate_weight_grad = lax.dynamic_slice_in_dim(all_cols[:, 3], me * (width // n), width // n, 1)

    dtokens = columns_to_tokens(dcols, 4, width)
    drates = columns_to_tokens(dpre, 1, HEADS)[:, 0]
    dnormed = dot_t(dtokens[:, :3].reshape(tokens, 3 * width), triple_weight) + dot_t(dtokens[:, 3], gate_weight)
    dnormed = dnormed + dot_t(drates, rate_weight)
    mixer_gain_part = jnp.sum(dnormed * xhat, axis=0)
    dxhat = dnormed * mixer_gain
    input_grad = dmiddle + inv * (dxhat - xhat * jnp.mean(dxhat * xhat, axis=-1, keepdims=True))

    head_parts = [
        rate_part.T,
        jnp.sum(dpre, axis=0)[:, None],
        gw1,
        gb1[:, 0],
        gw2.transpose(0, 2, 1),
        gb2[:, 0, :HEAD],
        jnp.sum(ggain, axis=1)[:, :HEAD],
        jnp.sum(gshift, axis=1)[:, :HEAD],
    ]
    shapes = [part.shape for part in head_parts]
    flat = jnp.concatenate([part.reshape(heads, -1) for part in head_parts], axis=1)
    size = flat.size
    flat = jnp.pad(flat.reshape(-1), (0, -size % (n_rows * LANES * 8))).reshape(n_rows, -1, LANES)
    flat = gather(scatter_sum(flat, "rows"), "rows").reshape(-1)[:size].reshape(heads, -1)
    flat = gather(flat, "seq").reshape(n * heads, -1)[:HEADS]
    head_grads = []
    start = 0
    for shape in shapes:
        count = 1
        for extent in shape[1:]:
            count *= extent
        head_grads.append(flat[:, start : start + count].reshape((HEADS,) + shape[1:]))
        start += count
    gains = sum_over(sum_over(jnp.stack([mixer_gain_part, feed_gain_part]), "seq"), "rows")

    return (
        layer_output[None],
        input_grad[None],
        gains[0],
        triple_weight_grad,
        head_grads[0].T,
        head_grads[1][:, 0],
        head_grads[2],
        head_grads[3],
        head_grads[4],
        head_grads[5],
        head_grads[6],
        head_grads[7],
        gate_weight_grad,
        output_weight_grad,
        gains[1],
        feed_weight_grad,
        down_weight_grad,
    )


def solution(mesh):
    tokens = P("rows", "seq", None)
    shard = P("rows", "seq")
    in_specs = (tokens, P("rows", None), tokens) + (P(),) * 15
    out_specs = (tokens, tokens, P(), shard) + (P(),) * 8 + (shard, shard, P(), shard, shard)
    return jax.shard_map(local, mesh=mesh, in_specs=in_specs, out_specs=out_specs, check_vma=False)
```

time: 4920 us -> 956 us (0.19)
  matrix products: 2230 us -> 84.5 us
  other arithmetic: 1140 us -> 84.8 us
  local copies, waits for them, and re-layouts: 783 us -> 121 us
  Pallas kernels: 0 us -> 432 us
  waiting for transfers between devices: 507 us -> 162 us
  loops' own time: 103 us -> 0 us
    dot_general x2130 -> x17, matrix products: 2230 us -> 84.5 us  [the longest x6 31.9 us: dot_t(): lax.dot_general(left, right, (((1,), (1,)), ((), ())), precision=high)]
    pallas_call x0 -> x2, Pallas kernels: none -> 432 us  [the longest x1 252 us: chain_backward(): pl.pallas_call(functools.partial(bwd_kernel, heads, steps), grid_spec=plt...]
    add x419 -> x25, other arithmetic: 442 us -> 24 us  [the longest x19 22.4 us: scatter_sum(): value = jnp.where(upper, upper_half, lower_half) + other]
    squeeze x448 -> x0, local copies, waits for them, and re-layouts: 415 us -> none  [one_row(): lax.scan(checked, unpack_state(row_start), row_features + (row_resets,))]
    reduce_scatter x7 -> x0, waiting for transfers between devices: 304 us -> none  [the longest x1 99.4 us: local(): lax.psum_scatter(post_grads[2], 'seq', scatter_dimension=1, tiled=True)]
    reduce_sum x786 -> x6, other arithmetic: 241 us -> 5.19 us  [the longest x1 1.42 us: local(): inv = lax.rsqrt(jnp.mean(x * x, axis=-1, keepdims=True) + EPS)]
    sub x256 -> x2, other arithmetic: 215 us -> 1.88 us  [the longest x1 1.81 us: local(): w2i = w2t - jnp.mean(w2t, axis=1, keepdims=True)]
    unnamed x14 -> x0, waiting for transfers between devices: 133 us -> none
where the time goes in v1:
time: 956 us; the launch traced here: 945 us
  Pallas kernels  432 us (45%)
  waiting for transfers between devices  162 us (17%)
  local copies, waits for them, and re-layouts  121 us (13%)
  other arithmetic  84.8 us (9%)
  matrix products  84.5 us (9%)
  starting transfers between devices  59.2 us (6%)
    pallas_call x1, Pallas kernels, chain_backward(): pl.pallas_call(functools.partial(bwd_kernel, heads, steps), grid_spec=plt...  252 us
    pallas_call x1, Pallas kernels, chain_forward(): pl.pallas_call(functools.partial(fwd_kernel, heads, steps), grid_spec=plt...  179 us
    ppermute x35, waiting for transfers between devices, swap(): lax.ppermute(value, axis, [(source, source ^ mask) for source in range(co...  152 us
    ppermute x35, starting transfers between devices, swap(): lax.ppermute(value, axis, [(source, source ^ mask) for source in range(co...  37.1 us
    unnamed x153, local copies, waits for them, and re-layouts  33.1 us
    dot_general x6, matrix products, dot_t(): lax.dot_general(left, right, (((1,), (1,)), ((), ())), precision=high)  31.9 us
    dot_general x6, matrix products, dot(): return jnp.dot(left, right, precision=high)  29.7 us
    dot_general x5, matrix products, t_dot(): lax.dot_general(left, right, (((0,), (0,)), ((), ())), precision=high)  22.9 us
  transfers between devices with their start and end apart: 40, of which 21 were waited for; matrix products, arithmetic and copies ran while one was open for 23% of the time, Pallas kernels for 27%

profile of v1, /device:TPU:0, one launch (start us, length us, event | category | flops | bytes accessed | tf_op | source)
XLA Modules:
  0.0 945.1 jit_solution(10775404860655571141)
XLA Ops:
  4.3 3.0 collective-permute-start
  8.1 8.2 copy.391
  18.3 6.8 collective-permute-done
  32.8 5.6 fusion.2.qkv_ref
  38.4 3.1 fusion.59
  41.5 2.4 copy.390
  43.9 2.5 copy.388
  46.4 4.2 broadcast_multiply_fusion
  53.1 179.3 %shard_map.305 = (f32[1024,256]{1,0:T(8,128)}, bf16[64,3,128,256]{3,2,1,0:T(8,128)(2,1)}, bf16[64,3,128,256]{3,2,1,0:T(8,128)(2,1)}, f32[64,3,16,256]{3,2,1,0:T(...) custom-call(s32[64]{0:T(128)} %convert_element_type.18.resets_ref, ...), custom_call_target="tpu_custom_call" | custom-call | tf_op jit(solution)/shard_map/pallas_call | solution.py:415
  232.4 2.5 slice_multiply_fusion.2
  234.9 2.4 copy.393
  237.3 4.5 all-to-all-start
  241.9 3.5 copy.401
  245.4 8.1 all-to-all-done
  253.6 3.2 multiply_reduce_fusion.4
  258.0 9.1 fusion.60
  267.1 8.7 add_multiply_fusion
  277.1 8.3 multiply_reduce_fusion
  289.4 3.9 fusion.63
  293.7 5.1 fusion.15
  298.8 4.2 all-to-all-start.1
  309.0 3.4 pad_maximum_fusion
  315.0 4.5 fusion.6
  323.5 3.7 bitcast_multiply_fusion.1
  328.4 252.3 %shard_map.306 = (f32[1024,640]{1,0:T(8,128)}, f32[1024,128]{1,0:T(8,128)}, f32[3,64,256]{2,1,0:T(8,128)}, f32[3,16,256]{2,1,0:T(8,128)}, f32[3,64,256]{2,1,0:T(...) custom-call(s32[64]{0:T(128)} %convert_element_type.18.resets_ref, ...), custom_call_target="tpu_custom_call" | custom-call | tf_op jit(solution)/shard_map/pallas_call | solution.py:438
  590.6 3.3 dynamic-update-slice.2
  595.3 2.8 dynamic-update-slice.4
  605.3 5.3 select_bitcast_fusion
  613.4 2.5 copy.520
  617.8 3.3 all-to-all-start.3
  622.0 2.7 collective-permute-start.14
  624.7 2.6 pad_maximum_fusion.3
  630.0 4.0 fusion
  636.8 3.6 copy.398
  641.0 5.1 all-to-all-start.2
  651.5 20.8 %collective-permute-done.17 = f32[2,2,104,128]{3,2,0,1:T(8,128)S(1)} collective-permute-done((f32[2,2,104,128]{3,2,0,1:T(8,128)S(1)}, f32[2,2,104,128]{3,2,0,1:T(8,128)S(1)}, u32[]{:S(2)}, u32[]{:S(2)}) %collective-permute-start.17) | collective-permute-done | bytes 213024 | tf_op jit(solution)/shard_map/ppermute | solution.py:473
  677.9 17.2 %collective-permute-done.18 = f32[3,33985]{1,0:T(4,128)S(1)} collective-permute-done((f32[3,33985]{1,0:T(4,128)}, f32[3,33985]{1,0:T(4,128)S(1)}, u32[]{:S(2)}, u32[]{:S(2)}) %collective-permute-start.18) | collective-permute-done | bytes 407852 | tf_op jit(solution)/shard_map/ppermute | solution.py:473
  696.8 10.5 %collective-permute-done.21 = f32[768,192]{0,1:T(8,128)S(1)} collective-permute-done((f32[768,192]{0,1:T(8,128)S(1)}, f32[768,192]{0,1:T(8,128)S(1)}, u32[]{:S(2)}, u32[]{:S(2)}) %collective-permute-start.21) | collective-permute-done | bytes 589856 | tf_op jit(solution)/shard_map/ppermute | solution.py:473
  708.2 3.0 reshape_reshape.31
  717.1 7.0 collective-permute-done.22
  727.7 6.0 collective-permute-done.23
  736.2 7.7 collective-permute-done.24
  748.7 3.4 collective-permute-start.9
  756.0 3.6 copy.441
  764.5 3.8 reshape_reshape.30
  768.3 3.6 fusion.52
  776.7 5.0 all-to-all-start.4
  784.0 9.1 fusion.62
  801.5 3.0 reshape.348
  804.5 2.7 copy.465
  810.1 19.7 %collective-permute-done.3 = f32[2,768]{1,0:T(2,128)S(1)} collective-permute-done((f32[2,768]{1,0:T(2,128)S(1)}, f32[2,768]{1,0:T(2,128)S(1)}, u32[]{:S(2)}, u32[]{:S(2)}) %collective-permute-start.3) | collective-permute-done | bytes 6176 | tf_op jit(solution)/shard_map/ppermute | solution.py:473
  834.5 2.8 collective-permute-done.5
  838.6 3.2 collective-permute-done.6
  841.8 4.7 bitcast_add_fusion
  849.6 8.3 fusion.64
  865.3 3.6 copy.411
  872.3 9.6 %collective-permute-done.31 = f32[2048,192]{0,1:T(8,128)} collective-permute-done((f32[2048,192]{0,1:T(8,128)}, f32[2048,192]{0,1:T(8,128)}, u32[]{:S(2)}, u32[]{:S(2)}) %collective-permute-start.31) | collective-permute-done | bytes 1572896 | tf_op jit(solution)/shard_map/ppermute | solution.py:473
  881.9 3.0 bitcast_add_fusion.1
  884.9 3.7 reshape_reshape.33
  888.6 3.7 fusion.53
  900.8 9.0 collective-permute-done.32
  913.7 6.1 collective-permute-done.28
  920.1 6.6 collective-permute-done.33
  927.5 14.4 %collective-permute-done.29 = f32[96,1024]{1,0:T(8,128)S(1)} collective-permute-done((f32[96,1024]{1,0:T(8,128)S(1)}, f32[96,1024]{1,0:T(8,128)S(1)}, u32[]{:S(2)}, u32[]{:S(2)}) %collective-permute-start.29) | collective-permute-done | bytes 393248 | tf_op jit(solution)/shard_map/ppermute | solution.py:473
  (355 shorter events, 160.5 us)
Async XLA Ops:
  0.7 37.7 %copy-start = (f32[768,768]{1,0:T(8,128)S(1)}, f32[768,768]{1,0:T(8,128)}, u32[]{:S(2)}) copy-start(f32[768,768]{1,0:T(8,128)} %param.31) | copy-start | bytes 7077892
  2.1 23.0 %copy-start.53 = (f32[256]{0:T(256)}, f32[256]{0:T(256)S(1)}, u32[]{:S(2)}) copy-start(f32[256]{0:T(256)S(1)} %add_rsqrt_fusion.1) | copy-start | bytes 3076
  4.3 20.8 %collective-permute-start = (f32[256,768]{1,0:T(8,128)}, f32[256,768]{1,0:T(8,128)}, u32[]{:S(2)}, u32[]{:S(2)}) collective-permute-start(f32[256,768]{1,0:T(8,128)} %fusion.26), channel_id=1, source_target_pairs={{0,2},{1,3},{2,0},{3,1},{4,6},{5,7},{6,4},{7,5},{8,10},{9,11},{10,... | collective-permute-start | bytes 2359304 | tf_op jit(solution)/shard_map/ppermute | solution.py:473
  8.1 17.0 %copy-start.8 = (f32[1,256,768]{2,1,0:T(8,128)S(1)}, f32[1,256,768]{2,1,0:T(8,128)}, u32[]{:S(2)}) copy-start(f32[1,256,768]{2,1,0:T(8,128)} %param.18) | copy-start | bytes 2359300
  8.1 17.0 %copy-start.49 = (f32[768]{0:T(1024)S(1)}, f32[768]{0:T(1024)}, u32[]{:S(2)}) copy-start(f32[768]{0:T(1024)} %param.21) | copy-start | bytes 9220
  26.6 5.4 collective-permute-start.1
  50.6 181.8 %copy-start.18 = (f32[1024,192]{1,0:T(8,128)S(1)}, f32[1024,192]{1,0:T(8,128)}, u32[]{:S(2)}) copy-start(f32[1024,192]{1,0:T(8,128)} %copy.390) | copy-start | bytes 2359300
  50.6 181.8 %copy-start.19 = (f32[1024,192]{1,0:T(8,128)S(1)}, f32[1024,192]{1,0:T(8,128)}, u32[]{:S(2)}) copy-start(f32[1024,192]{1,0:T(8,128)} %copy.388) | copy-start | bytes 2359300
  237.3 16.3 %all-to-all-start = ((f32[4,256,192]{1,2,0:T(8,128)}), f32[4,256,192]{1,2,0:T(8,128)}, u32[]{:S(2)}, u32[]{:S(2)}) async-start(f32[4,256,192]{1,2,0:T(8,128)} %copy.393), calls=%async_computation | async-start | bytes 1572864 | tf_op jit(solution)/shard_map/all_to_all | solution.py:514
  256.8 28.6 %copy-start.11 = (f32[256,768]{1,0:T(8,128)}, f32[256,768]{1,0:T(8,128)S(1)}, u32[]{:S(2)}) copy-start(f32[256,768]{1,0:T(8,128)S(1)} %get-tuple-element.213) | copy-start | bytes 2359300
  256.8 28.6 %copy-start.55 = (f32[256]{0:T(256)}, f32[256]{0:T(256)S(1)}, u32[]{:S(2)}) copy-start(f32[256]{0:T(256)S(1)} %add_rsqrt_fusion) | copy-start | bytes 3076
  258.0 19.1 %slice-start = ((s8[12582912]{0:T(1024)(128)(4,1)}), s8[4194304]{0:T(1024)(128)(4,1)S(1)}, s32[]{:S(2)}) async-start(s8[12582912]{0:T(1024)(128)(4,1)} %bitcast.420), calls=%async_computation.5 | async-start | bytes 8388608
  258.0 19.1 %slice-start.1 = ((s8[12582912]{0:T(1024)(128)(4,1)}), s8[4194304]{0:T(1024)(128)(4,1)S(1)}, s32[]{:S(2)}) async-start(s8[12582912]{0:T(1024)(128)(4,1)} %bitcast.420), calls=%async_computation.6 | async-start | bytes 8388608
  267.1 10.0 %slice-start.2 = ((s8[12582912]{0:T(1024)(128)(4,1)}), s8[4194304]{0:T(1024)(128)(4,1)S(1)}, s32[]{:S(2)}) async-start(s8[12582912]{0:T(1024)(128)(4,1)} %bitcast.420), calls=%async_computation.7 | async-start | bytes 8388608
  293.3 355.0 %collective-permute-start.25 = (f32[256,768]{1,0:T(8,128)}, f32[256,768]{1,0:T(8,128)}, u32[]{:S(2)}, u32[]{:S(2)}) collective-permute-start(f32[256,768]{1,0:T(8,128)} %multiply_multiply_fusion), channel_id=1, source_target_pairs={{0,2},{1,3},{2,0},{3,1},{4,6},{5,7},{6,4},{7,5},{8,10},{9,11},{10,... | collective-permute-start | bytes 2359304 | tf_op jit(solution)/shard_map/ppermute | solution.py:473
  298.8 22.3 %all-to-all-start.1 = ((f32[4,256,192]{1,2,0:T(8,128)}), f32[4,256,192]{1,2,0:T(8,128)}, u32[]{:S(2)}, u32[]{:S(2)}) async-start(f32[4,256,192]{1,2,0:T(8,128)} %bitcast.444), calls=%async_computation.1 | async-start | bytes 1572864 | tf_op jit(solution)/shard_map/all_to_all | solution.py:522
  307.7 367.0 %collective-permute-start.20 = (f32[2,768,192]{1,2,0:T(8,128)}, f32[2,768,192]{1,2,0:T(8,128)}, u32[]{:S(2)}, u32[]{:S(2)}) collective-permute-start(f32[2,768,192]{1,2,0:T(8,128)} %select_bitcast_fusion.7), channel_id=1, source_target_pairs={{0,1},{1,0},{2,3},{3,2},{4,5},{5,4},{6,7},{7,6},{8,9},{9,8},{10,11... | collective-permute-start | bytes 3538952 | tf_op jit(solution)/shard_map/ppermute | solution.py:473
  328.3 252.3 %copy-start.20 = (f32[1024,128]{1,0:T(8,128)S(1)}, f32[1024,128]{1,0:T(8,128)}, u32[]{:S(2)}) copy-start(f32[1024,128]{1,0:T(8,128)} %get-tuple-element.208.rate_ref) | copy-start | bytes 1572868
  328.3 252.3 %copy-start.41 = (f32[1024,128]{1,0:T(8,128)S(1)}, f32[1024,128]{1,0:T(8,128)}, u32[]{:S(2)}) copy-start(f32[1024,128]{1,0:T(8,128)} %get-tuple-element.209) | copy-start | bytes 1572868
  328.4 253.5 %copy-start.2 = (f32[2,2,256,768]{3,2,1,0:T(8,128)S(1)}, f32[2,2,256,768]{3,2,1,0:T(8,128)}, u32[]{:S(2)}) copy-start(f32[2,2,256,768]{3,2,1,0:T(8,128)} %copy-done.1) | copy-start | bytes 9437188
  603.5 7.1 collective-permute-start.12
  610.7 10.3 %collective-permute-start.13 = (f32[2,104,128]{2,1,0:T(8,128)S(1)}, f32[2,104,128]{2,1,0:T(8,128)}, u32[]{:S(2)}, u32[]{:S(2)}) collective-permute-start(f32[2,104,128]{2,1,0:T(8,128)S(1)} %select_bitcast_fusion.30), channel_id=1, source_target_pairs={{0,8},{4,12},{8,0},{12,4},{16,24},{20,28},{24,16},{28,20},{1,9},{5... | collective-permute-start | bytes 319496 | tf_op jit(solution)/shard_map/ppermute | solution.py:473
  615.9 225.9 %collective-permute-start.30 = (f32[2,2048,192]{1,2,0:T(8,128)}, f32[2,2048,192]{1,2,0:T(8,128)}, u32[]{:S(2)}, u32[]{:S(2)}) collective-permute-start(f32[2,2048,192]{1,2,0:T(8,128)} %select_bitcast_fusion), channel_id=1, source_target_pairs={{0,1},{1,0},{2,3},{3,2},{4,5},{5,4},{6,7},{7,6},{8,9},{9,8},{10,11... | collective-permute-start | bytes 9437192 | tf_op jit(solution)/shard_map/ppermute | solution.py:473
  617.8 23.2 %all-to-all-start.3 = ((f32[4,256,3]{1,2,0:T(4,128)}), f32[4,256,3]{1,2,0:T(4,128)S(1)}, u32[]{:S(2)}, u32[]{:S(2)}) async-start(f32[4,256,3]{1,2,0:T(4,128)} %copy.400), calls=%async_computation.3 | async-start | bytes 32768 | tf_op jit(solution)/shard_map/all_to_all | solution.py:514
  622.0 6.2 collective-permute-start.14
  628.2 5.8 collective-permute-start.15
  634.1 12.6 %collective-permute-start.16 = (f32[2,104,128]{2,1,0:T(8,128)S(1)}, f32[2,104,128]{2,1,0:T(8,128)S(1)}, u32[]{:S(2)}, u32[]{:S(2)}) collective-permute-start(f32[2,104,128]{2,1,0:T(8,128)S(1)} %pad_maximum_fusion.14), channel_id=1, source_target_pairs={{0,8},{4,12},{8,0},{12,4},{16,24},{20,28},{24,16},{28,20},{1,9},{5... | collective-permute-start | bytes 319496 | tf_op jit(solution)/shard_map/ppermute | solution.py:473
  640.4 74.5 %collective-permute-start.7 = (f32[2,2,96,768]{3,2,1,0:T(8,128)}, f32[2,2,96,768]{3,2,1,0:T(8,128)}, u32[]{:S(2)}, u32[]{:S(2)}) collective-permute-start(f32[2,2,96,768]{3,2,1,0:T(8,128)} %select_bitcast_fusion.8), channel_id=1, source_target_pairs={{0,4},{4,0},{8,12},{12,8},{16,20},{20,16},{24,28},{28,24},{1,5},{5... | collective-permute-start | bytes 3538952 | tf_op jit(solution)/shard_map/ppermute | solution.py:473
  641.0 135.7 %all-to-all-start.2 = ((f32[4,256,768]{1,2,0:T(8,128)}), f32[4,256,768]{1,2,0:T(8,128)}, u32[]{:S(2)}, u32[]{:S(2)}) async-start(f32[4,256,768]{1,2,0:T(8,128)} %copy.398), calls=%async_computation.2 | async-start | bytes 6291456 | tf_op jit(solution)/shard_map/all_to_all | solution.py:514
  646.7 25.5 %collective-permute-start.17 = (f32[2,2,104,128]{3,2,0,1:T(8,128)S(1)}, f32[2,2,104,128]{3,2,0,1:T(8,128)S(1)}, u32[]{:S(2)}, u32[]{:S(2)}) collective-permute-start(f32[2,2,104,128]{3,2,0,1:T(8,128)S(1)} %pad_maximum_fusion.13), channel_id=1, source_target_pairs={{0,4},{4,0},{8,12},{12,8},{16,20},{20,16},{24,28},{28,24},{1,5},{5... | collective-permute-start | bytes 638984 | tf_op jit(solution)/shard_map/ppermute | solution.py:473
  649.8 22.5 %copy-start.24 = (f32[1,256,768]{2,1,0:T(8,128)}, f32[1,256,768]{2,1,0:T(8,128)S(1)}, u32[]{:S(2)}) copy-start(f32[1,256,768]{2,1,0:T(8,128)S(1)} %get-tuple-element.174) | copy-start | bytes 2359300
  649.9 22.5 %copy-start.26 = (f32[1,256,768]{2,1,0:T(8,128)}, f32[1,256,768]{2,1,0:T(8,128)S(1)}, u32[]{:S(2)}) copy-start(f32[1,256,768]{2,1,0:T(8,128)S(1)} %get-tuple-element.175) | copy-start | bytes 2359300
  651.3 100.8 %collective-permute-start.26 = (f32[2,256,768]{2,1,0:T(8,128)}, f32[2,256,768]{2,1,0:T(8,128)}, u32[]{:S(2)}, u32[]{:S(2)}) collective-permute-start(f32[2,256,768]{2,1,0:T(8,128)} %pad_maximum_fusion.8), channel_id=1, source_target_pairs={{0,1},{1,0},{2,3},{3,2},{4,5},{5,4},{6,7},{7,6},{8,9},{9,8},{10,11... | collective-permute-start | bytes 4718600 | tf_op jit(solution)/shard_map/ppermute | solution.py:473
  673.5 21.6 %copy-start.40 = (f32[3,33985]{1,0:T(4,128)S(1)}, f32[3,33985]{1,0:T(4,128)}, u32[]{:S(2)}) copy-start(f32[3,33985]{1,0:T(4,128)} %reshape.346) | copy-start | bytes 1223464
  673.5 21.6 %collective-permute-start.18 = (f32[3,33985]{1,0:T(4,128)}, f32[3,33985]{1,0:T(4,128)S(1)}, u32[]{:S(2)}, u32[]{:S(2)}) collective-permute-start(f32[3,33985]{1,0:T(4,128)} %reshape.346), channel_id=1, source_target_pairs={{0,2},{1,3},{2,0},{3,1},{4,6},{5,7},{6,4},{7,5},{8,10},{9,11},{10,... | collective-permute-start | bytes 1223468 | tf_op jit(solution)/shard_map/ppermute | solution.py:473
  677.0 30.2 %collective-permute-start.21 = (f32[768,192]{0,1:T(8,128)S(1)}, f32[768,192]{0,1:T(8,128)S(1)}, u32[]{:S(2)}, u32[]{:S(2)}) collective-permute-start(f32[768,192]{0,1:T(8,128)S(1)} %select_bitcast_fusion.16), channel_id=1, source_target_pairs={{0,2},{1,3},{2,0},{3,1},{4,6},{5,7},{6,4},{7,5},{8,10},{9,11},{10,... | collective-permute-start | bytes 1769480 | tf_op jit(solution)/shard_map/ppermute | solution.py:473
  713.4 10.7 %collective-permute-start.22 = (f32[2,2,96,192]{2,1,0,3:T(2,128)S(1)}, f32[2,2,96,192]{2,1,0,3:T(2,128)S(1)}, u32[]{:S(2)}, u32[]{:S(2)}) collective-permute-start(f32[2,2,96,192]{2,1,0,3:T(2,128)S(1)} %bitcast.455), channel_id=1, source_target_pairs={{0,4},{4,0},{8,12},{12,8},{16,20},{20,16},{24,28},{28,24},{1,5},{5... | collective-permute-start | bytes 884744 | tf_op jit(solution)/shard_map/ppermute | solution.py:473
  717.1 9.9 %copy-start.16 = (f32[2,2,96,768]{3,2,1,0:T(8,128)}, f32[2,2,96,768]{3,2,1,0:T(8,128)S(1)}, u32[]{:S(2)}) copy-start(f32[2,2,96,768]{3,2,1,0:T(8,128)S(1)} %fusion.12) | copy-start | bytes 3538948
  724.4 10.2 %copy-start.36 = (f32[1,3,33985]{2,0,1:T(1,128)S(1)}, f32[1,3,33985]{2,0,1:T(1,128)}, u32[]{:S(2)}) copy-start(f32[1,3,33985]{2,0,1:T(1,128)} %copy.424) | copy-start | bytes 1223464
  724.7 9.0 collective-permute-start.23
  727.0 19.2 %collective-permute-start.8 = (f32[2,96,768]{2,1,0:T(8,128)}, f32[2,96,768]{2,1,0:T(8,128)}, u32[]{:S(2)}, u32[]{:S(2)}) collective-permute-start(f32[2,96,768]{2,1,0:T(8,128)} %select_bitcast_fusion.19), channel_id=1, source_target_pairs={{0,8},{4,12},{8,0},{12,4},{16,24},{20,28},{24,16},{28,20},{1,9},{5... | collective-permute-start | bytes 1769480 | tf_op jit(solution)/shard_map/ppermute | solution.py:473
  734.0 9.9 %collective-permute-start.24 = (f32[96,192]{0,1:T(8,128)S(1)}, f32[96,192]{0,1:T(8,128)S(1)}, u32[]{:S(2)}, u32[]{:S(2)}) collective-permute-start(f32[96,192]{0,1:T(8,128)S(1)} %bitcast.462), channel_id=1, source_target_pairs={{0,16},{4,20},{8,24},{12,28},{16,0},{20,4},{24,8},{28,12},{1,17},{... | collective-permute-start | bytes 221192 | tf_op jit(solution)/shard_map/ppermute | solution.py:473
  736.2 23.4 %collective-permute-start.19 = (f32[2,3,33985]{2,0,1:T(2,128)}, f32[2,3,33985]{2,0,1:T(2,128)}, u32[]{:S(2)}, u32[]{:S(2)}) collective-permute-start(f32[2,3,33985]{2,0,1:T(2,128)} %pad_maximum_fusion.10), channel_id=1, source_target_pairs={{0,1},{1,0},{2,3},{3,2},{4,5},{5,4},{6,7},{7,6},{8,9},{9,8},{10,11... | collective-permute-start | bytes 2446928 | tf_op jit(solution)/shard_map/ppermute | solution.py:473
  748.7 26.0 %collective-permute-start.9 = (f32[96,768]{1,0:T(8,128)}, f32[96,768]{1,0:T(8,128)}, u32[]{:S(2)}, u32[]{:S(2)}) collective-permute-start(f32[96,768]{1,0:T(8,128)} %select_bitcast_fusion.24), channel_id=1, source_target_pairs={{0,16},{4,20},{8,24},{12,28},{16,0},{20,4},{24,8},{28,12},{1,17},{... | collective-permute-start | bytes 884744 | tf_op jit(solution)/shard_map/ppermute | solution.py:473
  775.7 33.3 %collective-permute-start.10 = (f32[96,768]{1,0:T(8,128)S(1)}, f32[96,768]{1,0:T(8,128)}, u32[]{:S(2)}, u32[]{:S(2)}) collective-permute-start(f32[96,768]{1,0:T(8,128)S(1)} %bitcast_add_fusion.7), channel_id=1, source_target_pairs={{0,2},{1,3},{2,0},{3,1},{4,6},{5,7},{6,4},{7,5},{8,10},{9,11},{10,... | collective-permute-start | bytes 884744 | tf_op jit(solution)/shard_map/ppermute | solution.py:473
  776.7 72.9 %all-to-all-start.4 = ((f32[4,256,1024]{2,1,0:T(8,128)}), f32[4,256,1024]{2,1,0:T(8,128)}, u32[]{:S(2)}, u32[]{:S(2)}) async-start(f32[4,256,1024]{2,1,0:T(8,128)} %bitcast.425), calls=%async_computation.4 | async-start | bytes 8388608 | tf_op jit(solution)/shard_map/all_to_all | solution.py:522
  797.0 10.2 %collective-permute-start.2 = (f32[2,768]{1,0:T(2,128)S(1)}, f32[2,768]{1,0:T(2,128)S(1)}, u32[]{:S(2)}, u32[]{:S(2)}) collective-permute-start(f32[2,768]{1,0:T(2,128)S(1)} %pad_maximum_fusion.15), channel_id=1, source_target_pairs={{0,1},{1,0},{2,3},{3,2},{4,5},{5,4},{6,7},{7,6},{8,9},{9,8},{10,11... | collective-permute-start | bytes 18440 | tf_op jit(solution)/shard_map/ppermute | solution.py:473
  807.3 30.2 %copy-start.15 = (f32[256,768]{1,0:T(8,128)S(1)}, f32[256,768]{1,0:T(8,128)}, u32[]{:S(2)}) copy-start(f32[256,768]{1,0:T(8,128)} %copy-done.14) | copy-start | bytes 2359300
  807.3 30.2 %copy-start.37 = (f32[256,768]{1,0:T(8,128)S(1)}, f32[256,768]{1,0:T(8,128)}, u32[]{:S(2)}) copy-start(f32[256,768]{1,0:T(8,128)} %get-tuple-element.215) | copy-start | bytes 2359300
  807.3 22.6 %collective-permute-start.3 = (f32[2,768]{1,0:T(2,128)S(1)}, f32[2,768]{1,0:T(2,128)S(1)}, u32[]{:S(2)}, u32[]{:S(2)}) collective-permute-start(f32[2,768]{1,0:T(2,128)S(1)} %fusion.46), channel_id=1, source_target_pairs={{0,2},{1,3},{2,0},{3,1},{4,6},{5,7},{6,4},{7,5},{8,10},{9,11},{10,... | collective-permute-start | bytes 18440 | tf_op jit(solution)/shard_map/ppermute | solution.py:473
  810.1 23.5 %copy-start.38 = (f32[1,96,768]{2,1,0:T(8,128)}, f32[1,96,768]{2,1,0:T(8,128)S(1)}, u32[]{:S(2)}) copy-start(f32[1,96,768]{2,1,0:T(8,128)S(1)} %get-tuple-element.189) | copy-start | bytes 884740
  829.9 3.7 collective-permute-start.4
  833.6 3.6 collective-permute-start.5
  834.5 27.1 %collective-permute-start.11 = (f32[2,96,768]{2,1,0:T(8,128)}, f32[2,96,768]{2,1,0:T(8,128)}, u32[]{:S(2)}, u32[]{:S(2)}) collective-permute-start(f32[2,96,768]{2,1,0:T(8,128)} %pad_maximum_fusion.11), channel_id=1, source_target_pairs={{0,1},{1,0},{2,3},{3,2},{4,5},{5,4},{6,7},{7,6},{8,9},{9,8},{10,11... | collective-permute-start | bytes 1769480 | tf_op jit(solution)/shard_map/ppermute | solution.py:473
  837.2 4.5 collective-permute-start.6
  848.6 33.3 %collective-permute-start.31 = (f32[2048,192]{0,1:T(8,128)}, f32[2048,192]{0,1:T(8,128)}, u32[]{:S(2)}, u32[]{:S(2)}) collective-permute-start(f32[2048,192]{0,1:T(8,128)} %select_bitcast_fusion.1), channel_id=1, source_target_pairs={{0,2},{1,3},{2,0},{3,1},{4,6},{5,7},{6,4},{7,5},{8,10},{9,11},{10,... | collective-permute-start | bytes 4718600 | tf_op jit(solution)/shard_map/ppermute | solution.py:473
  860.1 34.9 %collective-permute-start.27 = (f32[2,2,96,1024]{3,2,1,0:T(8,128)}, f32[2,2,96,1024]{3,2,1,0:T(8,128)}, u32[]{:S(2)}, u32[]{:S(2)}) collective-permute-start(f32[2,2,96,1024]{3,2,1,0:T(8,128)} %select_bitcast_fusion.2), channel_id=1, source_target_pairs={{0,4},{4,0},{8,12},{12,8},{16,20},{20,16},{24,28},{28,24},{1,5},{5... | collective-permute-start | bytes 4718600 | tf_op jit(solution)/shard_map/ppermute | solution.py:473
  871.2 13.7 %copy-start.31 = (f32[96,4,768]{2,0,1:T(8,128)}, f32[96,4,768]{2,0,1:T(8,128)S(1)}, u32[]{:S(2)}) copy-start(f32[96,4,768]{2,0,1:T(8,128)S(1)} %reshape.341) | copy-start | bytes 3538948
  871.2 10.7 %copy-start.6 = (f32[2,2048,192]{1,2,0:T(8,128)S(1)}, f32[2,2048,192]{1,2,0:T(8,128)}, u32[]{:S(2)}) copy-start(f32[2,2048,192]{1,2,0:T(8,128)} %copy-done.5) | copy-start | bytes 9437188
  892.7 17.2 %collective-permute-start.32 = (f32[2,2,256,192]{2,1,0,3:T(2,128)S(1)}, f32[2,2,256,192]{2,1,0,3:T(2,128)S(1)}, u32[]{:S(2)}, u32[]{:S(2)}) collective-permute-start(f32[2,2,256,192]{2,1,0,3:T(2,128)S(1)} %bitcast.451), channel_id=1, source_target_pairs={{0,4},{4,0},{8,12},{12,8},{16,20},{20,16},{24,28},{28,24},{1,5},{5... | collective-permute-start | bytes 2359304 | tf_op jit(solution)/shard_map/ppermute | solution.py:473
  897.0 22.7 %collective-permute-start.28 = (f32[2,96,1024]{2,1,0:T(8,128)S(1)}, f32[2,96,1024]{2,1,0:T(8,128)S(1)}, u32[]{:S(2)}, u32[]{:S(2)}) collective-permute-start(f32[2,96,1024]{2,1,0:T(8,128)S(1)} %select_bitcast_fusion.11), channel_id=1, source_target_pairs={{0,8},{4,12},{8,0},{12,4},{16,24},{20,28},{24,16},{28,20},{1,9},{5... | collective-permute-start | bytes 2359304 | tf_op jit(solution)/shard_map/ppermute | solution.py:473
  911.5 15.1 %collective-permute-start.33 = (f32[2,256,192]{1,0,2:T(2,128)S(1)}, f32[2,256,192]{1,0,2:T(2,128)S(1)}, u32[]{:S(2)}, u32[]{:S(2)}) collective-permute-start(f32[2,256,192]{1,0,2:T(2,128)S(1)} %bitcast.454), channel_id=1, source_target_pairs={{0,8},{4,12},{8,0},{12,4},{16,24},{20,28},{24,16},{28,20},{1,9},{5... | collective-permute-start | bytes 1179656 | tf_op jit(solution)/shard_map/ppermute | solution.py:473
  920.0 21.9 %collective-permute-start.29 = (f32[96,1024]{1,0:T(8,128)S(1)}, f32[96,1024]{1,0:T(8,128)S(1)}, u32[]{:S(2)}, u32[]{:S(2)}) collective-permute-start(f32[96,1024]{1,0:T(8,128)S(1)} %select_bitcast_fusion.21), channel_id=1, source_target_pairs={{0,16},{4,20},{8,24},{12,28},{16,0},{20,4},{24,8},{28,12},{1,17},{... | collective-permute-start | bytes 1179656 | tf_op jit(solution)/shard_map/ppermute | solution.py:473
  927.4 16.6 %collective-permute-start.34 = (f32[256,192]{0,1:T(8,128)S(1)}, f32[256,192]{0,1:T(8,128)S(1)}, u32[]{:S(2)}, u32[]{:S(2)}) collective-permute-start(f32[256,192]{0,1:T(8,128)S(1)} %bitcast.460), channel_id=1, source_target_pairs={{0,16},{4,20},{8,24},{12,28},{16,0},{20,4},{24,8},{28,12},{1,17},{... | collective-permute-start | bytes 589832 | tf_op jit(solution)/shard_map/ppermute | solution.py:473
  (45 other events, 202.2 us)
